TPU v7x, 32 devices: a whole 2x2x4 slice. The times are simulated.
32 devices in a mesh: dp: 16 (over z, y, core), fsdp: 2 (over x).
Axes of the slice: x: 2, y: 2, z: 4, core: 2. Of those that a mesh axis runs over, the one named last changes fastest.
Arguments:
- pixels: bfloat16 [32768, 640], P(('dp', 'fsdp')), may hold values from -6 to 6
- wave_table: float32 [16], replicated, may hold values from 0.4 to 2.5
- band_count: int32 [7], replicated, may hold values from 3 to 10, as said below
- wave_index: int32 [7, 10], replicated, may hold values from 0 to 15
- group_sensor: int32 [16], replicated, may hold values from 0 to 6
- chip_kind: int32 [32], P(('dp', 'fsdp')), may hold values from 0 to 1
- chip_gsd: int32 [32, 4], P(('dp', 'fsdp')), may hold values from 1 to 30
- time_loc: float32 [32, 4, 8], P(('dp', 'fsdp')), may hold values from -1 to 1
- gen_in: bfloat16 [128, 128], replicated, may hold values from -0.5 to 0.5
- gen_bias: bfloat16 [128], replicated, may hold values from -3 to 3
- gen_out: bfloat16 [128, 49920], P(None, ('dp', 'fsdp')), may hold values from -0.0390625 to 0.0390625
- meta_weight: bfloat16 [9, 768], replicated, may hold values from -3 to 3
- w_qkv: bfloat16 [768, 2304], P('dp', 'fsdp'), may hold values from -0.21875 to 0.21875
- w_out: bfloat16 [768, 768], P('dp', 'fsdp'), may hold values from -0.875 to 0.875
- w_up: bfloat16 [768, 3072], P('dp', 'fsdp'), may hold values from -0.21875 to 0.21875
- w_down: bfloat16 [3072, 768], P('dp', 'fsdp'), may hold values from -0.109375 to 0.109375
- vectors: bfloat16 [768, 6], P('dp')
- b_up: bfloat16 [3072], P('dp'), may hold values from -2 to 2
- cotangent: bfloat16 [33024, 768], P(('dp', 'fsdp')), may hold values from -6 to 6
Outputs:
- layer_out: bfloat16 [33024, 768], P(('dp', 'fsdp'))
- pixel_grad: float32 [32768, 640], P(('dp', 'fsdp'))
- gen_in_grad: float32 [128, 128], replicated
- gen_bias_grad: float32 [128], replicated
- gen_out_grad: float32 [128, 49920], P(None, ('dp', 'fsdp'))
- meta_grad: float32 [9, 768], replicated
- w_qkv_grad: float32 [768, 2304], P('dp', 'fsdp')
- w_out_grad: float32 [768, 768], P('dp', 'fsdp')
- w_up_grad: float32 [768, 3072], P('dp', 'fsdp')
- w_down_grad: float32 [3072, 768], P('dp', 'fsdp')
- vectors_grad: float32 [768, 6], P('dp')
- b_up_grad: float32 [3072], P('dp')
Inputs may be any that keep to these rules, and one draw needn't show every extreme that they name: `band_count`: one sensor has exactly 10 bands.
All inputs are finite; a program needn't handle non-finite values.
Results may differ from a plain program's by a relative error of at most 0.019.
Values may be sent and summed in bfloat16 or wider, within the bound.
A program may use at most 320 MiB of HBM per device.

v0:
```python
import math

import jax
import jax.numpy as jnp
from jax import lax
from jax.sharding import PartitionSpec as P

D = 768
HEADS = 12
HEAD = 64
GEN = 128
PIX = 64
MAXB = 10
SENSORS = 7
TOK_DEV = 1024
SLOTS = 4
GENOUT = 49920


def exact_dot(left, right):
    return jnp.dot(left, right, precision=lax.Precision.HIGHEST)


def inner_dot(left, right):
    return lax.dot_general(
        left, right, (((0,), (0,)), ((), ())), preferred_element_type=jnp.float32
    )


def outer_dot(left, right):
    return lax.dot_general(
        left, right, (((1,), (1,)), ((), ())), preferred_element_type=jnp.float32
    )


def gelu_exact(values):
    return jax.nn.gelu(values, approximate=False)


def gelu_slope(values, upstream):
    return jax.vjp(gelu_exact, values)[1](upstream)[0]


def table_lookup(indices, table):
    return jnp.sum(
        jnp.where(
            indices[:, None] == jnp.arange(table.shape[0], dtype=jnp.int32)[None, :],
            table[None, :],
            0.0,
        ),
        axis=1,
    )


def wave_code(wavelengths):
    half = GEN // 2
    omega = 1.0 / 10000.0 ** (jnp.arange(half, dtype=jnp.float32) / half)
    angle = (wavelengths * 1000.0)[:, None] * omega[None, :]
    return jnp.concatenate([jnp.sin(angle), jnp.cos(angle)], axis=1)


def place_code(kind_one, gsd_one):
    small = TOK_DEV // SLOTS
    index = jnp.arange(TOK_DEV, dtype=jnp.int32)
    within = jnp.where(kind_one == 1, index, index % small)
    side = jnp.where(kind_one == 1, math.isqrt(TOK_DEV), math.isqrt(small)).astype(jnp.int32)
    across = (within // side).astype(jnp.float32)
    along = (within % side).astype(jnp.float32)
    holder = jnp.where(kind_one == 1, 0, index // small)
    ground = (
        jnp.sum(
            jnp.where(
                holder[:, None] == jnp.arange(SLOTS, dtype=jnp.int32)[None, :], gsd_one[None, :], 0
            ),
            axis=1,
        ).astype(jnp.float32)
        / 10.0
    )
    quarter = D // 4
    omega = 1.0 / 10000.0 ** (jnp.arange(quarter, dtype=jnp.float32) / (quarter - 1))
    first = (across * ground)[:, None] * omega[None, :]
    second = (along * ground)[:, None] * omega[None, :]
    return jnp.concatenate(
        [jnp.sin(first), jnp.cos(first), jnp.sin(second), jnp.cos(second)], axis=1
    )


def segment_ids(kind_one):
    index = jnp.arange(TOK_DEV, dtype=jnp.int32)
    patches = jnp.where(kind_one == 1, 0, index // (TOK_DEV // SLOTS))
    extra = jnp.arange(2 * SLOTS, dtype=jnp.int32) // 2
    return jnp.concatenate([patches, extra])


def layer_norm(values, gain, shift):
    centred = values - jnp.mean(values, axis=-1, keepdims=True)
    scale = lax.rsqrt(jnp.mean(centred * centred, axis=-1, keepdims=True) + 1e-05)
    normed = centred * scale
    return (normed * gain + shift, normed, scale)


def norm_back(upstream, normed, scale, gain):
    gain_grad = jnp.sum(upstream * normed, axis=0)
    shift_grad = jnp.sum(upstream, axis=0)
    scaled = upstream * gain
    inside = (
        scaled
        - jnp.mean(scaled, axis=-1, keepdims=True)
        - normed * jnp.mean(scaled * normed, axis=-1, keepdims=True)
    )
    return (scale * inside, gain_grad, shift_grad)


def body(
    pixels,
    wave_table,
    band_count,
    wave_index,
    group_sensor,
    chip_kind,
    chip_gsd,
    time_loc,
    gen_in,
    gen_bias,
    gen_out,
    meta_weight,
    w_qkv,
    w_out,
    w_up,
    w_down,
    vectors,
    b_up,
    cotangent,
):
    half_type = jnp.bfloat16
    group = lax.axis_index("dp")
    sensor = jnp.sum(
        jnp.where(jnp.arange(group_sensor.shape[0], dtype=jnp.int32) == group, group_sensor, 0)
    )
    chosen_sensor = jnp.arange(SENSORS, dtype=jnp.int32) == sensor
    band_total = jnp.sum(jnp.where(chosen_sensor, band_count, 0))
    gen_in_full = gen_in.astype(jnp.float32)
    gen_bias_full = gen_bias.astype(jnp.float32)
    codes = wave_code(table_lookup(wave_index.reshape(-1), wave_table))
    before = exact_dot(codes, gen_in_full) + gen_bias_full
    hidden = gelu_exact(before).astype(half_type)
    shard_made = jnp.dot(hidden, gen_out, preferred_element_type=jnp.float32).astype(half_type)
    all_made = lax.all_gather(shard_made, ("dp", "fsdp"), axis=1, tiled=True)
    generated = lax.dynamic_slice_in_dim(all_made, sensor * MAXB, MAXB, 0)
    live_band = (jnp.arange(MAXB, dtype=jnp.int32) < band_total)[:, None]
    kernel = jnp.where(live_band, generated[:, : PIX * D], jnp.zeros((), half_type)).reshape(
        MAXB * PIX, D
    )
    band_float = band_total.astype(jnp.float32)
    embed_bias = (
        jnp.sum(jnp.where(live_band, generated[:, PIX * D :].astype(jnp.float32), 0.0), axis=0)
        / band_float
    )
    kind_one = chip_kind[0]
    patches = (
        jnp.dot(pixels, kernel, preferred_element_type=jnp.float32)
        + embed_bias
        + place_code(kind_one, chip_gsd[0])
    )
    meta_full = meta_weight.astype(jnp.float32)
    stamps = exact_dot(time_loc[0], meta_full[1:])
    classes = jnp.broadcast_to(meta_full[0], stamps.shape)
    extra = jnp.stack([classes, stamps], axis=1).reshape(2 * SLOTS, D)
    tokens_in = jnp.concatenate([patches, extra], axis=0)
    total_rows = tokens_in.shape[0]
    qkv_rows, out_rows, up_rows, down_rows, vectors_all, b_up_all = (
        lax.all_gather(w_qkv, "dp", axis=0, tiled=True),
        lax.all_gather(w_out, "dp", axis=0, tiled=True),
        lax.all_gather(w_up, "dp", axis=0, tiled=True),
        lax.all_gather(w_down, "dp", axis=0, tiled=True),
        lax.all_gather(vectors, "dp", axis=0, tiled=True),
        lax.all_gather(b_up, "dp", axis=0, tiled=True),
    )
    w_qkv_all, w_out_all, w_up_all, w_down_all = (
        lax.all_gather(qkv_rows, "fsdp", axis=1, tiled=True),
        lax.all_gather(out_rows, "fsdp", axis=1, tiled=True),
        lax.all_gather(up_rows, "fsdp", axis=1, tiled=True),
        lax.all_gather(down_rows, "fsdp", axis=1, tiled=True),
    )
    vector_full = vectors_all.astype(jnp.float32)
    b_up_full = b_up_all.astype(jnp.float32)
    first_norm, normed_one, scale_one = layer_norm(tokens_in, vector_full[:, 0], vector_full[:, 1])
    first = first_norm.astype(half_type)
    qkv = jnp.dot(first, w_qkv_all, preferred_element_type=jnp.float32).astype(half_type)
    query = qkv[:, :D].reshape(total_rows, HEADS, HEAD)
    keys = qkv[:, D : 2 * D].reshape(total_rows, HEADS, HEAD)
    values = qkv[:, 2 * D :].reshape(total_rows, HEADS, HEAD)
    segment = segment_ids(kind_one)
    same = (segment[:, None] == segment[None, :])[None]
    scores = jnp.einsum("qhd,khd->hqk", query, keys, preferred_element_type=jnp.float32) * HEAD ** (
        -0.5
    )
    scores = jnp.where(same, scores, -1e30)
    peak = jnp.max(scores, axis=-1, keepdims=True)
    expo = jnp.exp(scores - peak)
    totals = jnp.sum(expo, axis=-1, keepdims=True)
    prob_half = (expo / totals).astype(half_type)
    mixed = (
        jnp.einsum("hqk,khd->qhd", prob_half, values, preferred_element_type=jnp.float32)
        .reshape(total_rows, D)
        .astype(half_type)
    )
    after = tokens_in + (
        jnp.dot(mixed, w_out_all, preferred_element_type=jnp.float32) + vector_full[:, 2]
    )
    second_norm, normed_two, scale_two = layer_norm(after, vector_full[:, 3], vector_full[:, 4])
    second = second_norm.astype(half_type)
    upper = jnp.dot(second, w_up_all, preferred_element_type=jnp.float32) + b_up_full
    active = gelu_exact(upper).astype(half_type)
    layer_out = (
        after + jnp.dot(active, w_down_all, preferred_element_type=jnp.float32) + vector_full[:, 5]
    ).astype(half_type)
    grad_top = cotangent.astype(jnp.float32)
    w_down_grad = inner_dot(active, cotangent)
    down_bias_grad = jnp.sum(grad_top, axis=0)
    d_active = outer_dot(cotangent, w_down_all)
    d_upper = gelu_slope(upper, d_active).astype(half_type)
    w_up_grad = inner_dot(second, d_upper)
    b_up_grad = jnp.sum(d_upper.astype(jnp.float32), axis=0)
    d_second = outer_dot(d_upper, w_up_all)
    d_after_norm, gain_two_grad, shift_two_grad = norm_back(
        d_second, normed_two, scale_two, vector_full[:, 3]
    )
    d_after = grad_top + d_after_norm
    d_proj = d_after.astype(half_type)
    w_out_grad = inner_dot(mixed, d_proj)
    out_bias_grad = jnp.sum(d_proj.astype(jnp.float32), axis=0)
    d_mixed = outer_dot(d_proj, w_out_all).astype(half_type).reshape(total_rows, HEADS, HEAD)
    again = jnp.einsum("qhd,khd->hqk", query, keys, preferred_element_type=jnp.float32) * HEAD ** (
        -0.5
    )
    again = jnp.where(same, again, -1e30)
    prob_full = jnp.exp(again - peak) / totals
    recalled = prob_full.astype(half_type)
    d_values = jnp.einsum("hqk,qhd->khd", recalled, d_mixed, preferred_element_type=jnp.float32)
    d_prob = jnp.einsum("qhd,khd->hqk", d_mixed, values, preferred_element_type=jnp.float32)
    d_scores = prob_full * (d_prob - jnp.sum(d_prob * prob_full, axis=-1, keepdims=True))
    d_scores = jnp.where(same, d_scores, 0.0).astype(half_type)
    d_query = jnp.einsum(
        "hqk,khd->qhd", d_scores, keys, preferred_element_type=jnp.float32
    ) * HEAD ** (-0.5)
    d_keys = jnp.einsum(
        "hqk,qhd->khd", d_scores, query, preferred_element_type=jnp.float32
    ) * HEAD ** (-0.5)
    d_qkv = jnp.concatenate(
        [
            d_query.reshape(total_rows, D),
            d_keys.reshape(total_rows, D),
            d_values.reshape(total_rows, D),
        ],
        axis=1,
    ).astype(half_type)
    w_qkv_grad = inner_dot(first, d_qkv)
    d_first = outer_dot(d_qkv, w_qkv_all)
    d_tokens_norm, gain_one_grad, shift_one_grad = norm_back(
        d_first, normed_one, scale_one, vector_full[:, 0]
    )
    d_tokens = (d_after + d_tokens_norm).astype(half_type)
    vectors_grad = jnp.stack(
        [
            gain_one_grad,
            shift_one_grad,
            out_bias_grad,
            gain_two_grad,
            shift_two_grad,
            down_bias_grad,
        ],
        axis=1,
    )
    d_patches = d_tokens[:TOK_DEV]
    d_extra = d_tokens[TOK_DEV:].astype(jnp.float32).reshape(SLOTS, 2, D)
    pixel_grad = outer_dot(d_patches, kernel)
    class_grad = jnp.sum(d_extra[:, 0], axis=0)
    stamp_grad = exact_dot(time_loc[0].T, d_extra[:, 1])
    meta_part = jnp.concatenate([class_grad[None, :], stamp_grad], axis=0)
    d_kernel = inner_dot(pixels, d_patches).reshape(MAXB, PIX * D)
    d_kernel = jnp.where(live_band, d_kernel, 0.0)
    d_bias = jnp.sum(d_patches.astype(jnp.float32), axis=0) / band_float
    d_bias_rows = jnp.where(live_band, d_bias[None, :], 0.0)
    d_generated = jnp.concatenate([d_kernel, d_bias_rows], axis=1).astype(half_type)
    placed = jnp.where(
        chosen_sensor[:, None, None], d_generated.astype(jnp.float32)[None], 0.0
    ).reshape(SENSORS * MAXB, GENOUT)
    columns = lax.psum_scatter(placed, ("dp", "fsdp"), scatter_dimension=1, tiled=True)
    gen_out_grad = exact_dot(hidden.astype(jnp.float32).T, columns)
    d_hidden = exact_dot(columns, gen_out.astype(jnp.float32).T)
    d_before = gelu_slope(before, d_hidden)
    gen_in_part = exact_dot(codes.T, d_before)
    gen_bias_part = jnp.sum(d_before, axis=0)
    meta_grad, gen_in_grad, gen_bias_grad = lax.psum(
        (meta_part, gen_in_part, gen_bias_part), ("dp", "fsdp")
    )
    qkv_cols, out_cols, up_cols, down_cols = (
        lax.psum_scatter(
            w_qkv_grad.astype(jnp.bfloat16), "fsdp", scatter_dimension=1, tiled=True
        ).astype(jnp.float32),
        lax.psum_scatter(
            w_out_grad.astype(jnp.bfloat16), "fsdp", scatter_dimension=1, tiled=True
        ).astype(jnp.float32),
        lax.psum_scatter(
            w_up_grad.astype(jnp.bfloat16), "fsdp", scatter_dimension=1, tiled=True
        ).astype(jnp.float32),
        lax.psum_scatter(
            w_down_grad.astype(jnp.bfloat16), "fsdp", scatter_dimension=1, tiled=True
        ).astype(jnp.float32),
    )
    vectors_group, b_up_group = lax.psum((vectors_grad, b_up_grad), "fsdp")
    w_qkv_out, w_out_out, w_up_out, w_down_out, vectors_out, b_up_out = (
        lax.psum_scatter(
            qkv_cols.astype(jnp.bfloat16), "dp", scatter_dimension=0, tiled=True
        ).astype(jnp.float32),
        lax.psum_scatter(
            out_cols.astype(jnp.bfloat16), "dp", scatter_dimension=0, tiled=True
        ).astype(jnp.float32),
        lax.psum_scatter(
            up_cols.astype(jnp.bfloat16), "dp", scatter_dimension=0, tiled=True
        ).astype(jnp.float32),
        lax.psum_scatter(
            down_cols.astype(jnp.bfloat16), "dp", scatter_dimension=0, tiled=True
        ).astype(jnp.float32),
        lax.psum_scatter(
            vectors_group.astype(jnp.bfloat16), "dp", scatter_dimension=0, tiled=True
        ).astype(jnp.float32),
        lax.psum_scatter(
            b_up_group.astype(jnp.bfloat16), "dp", scatter_dimension=0, tiled=True
        ).astype(jnp.float32),
    )
    return (
        layer_out,
        pixel_grad,
        gen_in_grad,
        gen_bias_grad,
        gen_out_grad,
        meta_grad,
        w_qkv_out,
        w_out_out,
        w_up_out,
        w_down_out,
        vectors_out,
        b_up_out,
    )


def solution(mesh):
    placed = (
        P(("dp", "fsdp"), None),
        P(),
        P(),
        P(),
        P(),
        P(("dp", "fsdp")),
        P(("dp", "fsdp"), None),
        P(("dp", "fsdp"), None, None),
        P(),
        P(),
        P(None, ("dp", "fsdp")),
        P(),
        P("dp", "fsdp"),
        P("dp", "fsdp"),
        P("dp", "fsdp"),
        P("dp", "fsdp"),
        P("dp", None),
        P("dp"),
        P(("dp", "fsdp"), None),
    )
    return jax.shard_map(
        body,
        mesh=mesh,
        in_specs=placed,
        out_specs=(
            P(("dp", "fsdp"), None),
            P(("dp", "fsdp"), None),
            P(),
            P(),
            P(None, ("dp", "fsdp")),
            P(),
            P("dp", "fsdp"),
            P("dp", "fsdp"),
            P("dp", "fsdp"),
            P("dp", "fsdp"),
            P("dp", None),
            P("dp"),
        ),
        check_vma=False,
    )
```

profile of v0, /device:TPU:0, one launch (start us, length us, event | category | flops | bytes accessed | tf_op | source)
XLA Modules:
  0.0 1549.7 jit_solution(2437010112335162297)
XLA Ops:
  16.5 36.8 %all-gather.11.cloned.1.call-done = bf16[768,1152]{1,0:T(8,128)(2,1)} async-done(((bf16[48,1152]{1,0:T(8,128)(2,1)}), bf16[768,1152]{1,0:T(8,128)(2,1)}) %all-gather.11.cloned.1.call-update) | async-done | bytes 1769488 | tf_op jit(solution)/shard_map/all_gather | solution.py:172
  53.4 22.5 %all_gather.37 = bf16[768,384]{1,0:T(8,128)(2,1)} all-gather(bf16[48,384]{1,0:T(8,128)(2,1)S(1)} %copy-done.35), channel_id=1, replica_groups=mesh['dp'=16,'fsdp'=2] {'dp'}, dimensions={0}, use_global_device_ids=true | all-gather | bytes 626688 | tf_op jit(solution)/shard_map/all_gather | solution.py:173
  75.9 21.3 %all-gather.17.cloned.1.call-done = bf16[768,1536]{1,0:T(8,128)(2,1)} async-done(((bf16[48,1536]{1,0:T(8,128)(2,1)}), bf16[768,1536]{1,0:T(8,128)(2,1)}) %all-gather.17.cloned.1.call-update) | async-done | bytes 2359312 | tf_op jit(solution)/shard_map/all_gather | solution.py:174
  102.8 32.6 %all-reduce = bf16[3072]{0:T(1024)(128)(2,1)S(1)} all-reduce(bf16[3072]{0:T(1024)(128)(2,1)S(1)} %dynamic-update-slice), channel_id=1, replica_groups=mesh['dp'=16,'fsdp'=2] {'dp'}, use_global_device_ids=true, to_apply=%add | all-reduce | flops 3072 | bytes 12288
  166.0 51.7 %all-gather.25.cloned.1.call-done = bf16[32,1560,70]{1,2,0:T(8,128)(2,1)} async-done(((bf16[1,1560,70]{1,2,0:T(8,128)(2,1)}), bf16[32,1560,70]{1,2,0:T(8,128)(2,1)}) %all-gather.25.cloned.1.call-update) | async-done | bytes 6988816 | tf_op jit(solution)/shard_map/all_gather | solution.py:148
  248.1 19.0 %all-gather.13.cloned.1.call-done = bf16[768,2304]{1,0:T(8,128)(2,1)} async-done(((bf16[768,1152]{1,0:T(8,128)(2,1)}), bf16[768,2304]{1,0:T(8,128)(2,1)}) %all-gather.13.cloned.1.call-update) | async-done | bytes 3538960 | tf_op jit(solution)/shard_map/all_gather | solution.py:180
  284.9 30.0 %fusion.105 = (f32[12,1032]{1,0:T(8,128)}, f32[12,1032,1032]{1,2,0:T(8,128)}) fusion(bf16[1032,12,64]{0,2,1:T(8,128)(2,1)} %bitcast.97, bf16[1032,12,64]{0,2,1:T(8,128)(2,1)} %bitcast.99, pred[1032,1032]{0,1:T(8,128)(4,1)} %broadcast_compare_fusion), kind=kOutput, calls=%fused_computation.209 | convolution fusion | flops 1686999040 | bytes 55406016 | tf_op jit(solution)/shard_map/sub | solution.py:200
  314.9 20.6 %fusion.41 = bf16[12,64,1032]{2,1,0:T(8,128)(2,1)} fusion(bf16[1032,12,64]{0,2,1:T(8,128)(2,1)S(1)} %bitcast.90, f32[12,1032,1032]{1,2,0:T(8,128)} %get-tuple-element.109, f32[12,1032]{1,0:T(8,128)} %get-tuple-element.108), kind=kOutput, calls=%fused_computation.67 | convolution fusion | flops 1662230016 | bytes 54340992 | tf_op jit(solution)/shard_map/hqk,khd->qhd/dot_general | solution.py:204
  355.5 39.6 %multiply_convert_fusion = (bf16[1032,3072]{1,0:T(8,128)(2,1)}, f32[1032,3072]{1,0:T(8,128)}, f32[1032,3072]{1,0:T(8,128)}) fusion(f32[3072]{0:T(1024)S(1)} %convert_element_type.178, bf16[768,3072]{1,0:T(8,128)(2,1)} %all-gather.19.cloned.1.call-done, f32[1032,768]{0,1:T(8,128)} %copy-done.2, f32[768]{0:T(1024)S(1)} %get-tuple-element.79, ...), kind=kOutput, calls=%fused_computation.24 | convolution fusion | flops 5082789888 | bytes 39618624 | tf_op jit(solution)/shard_map/dot_general | solution.py:213
  395.1 24.7 %all-gather.23.cloned.1.call-done = bf16[3072,768]{1,0:T(8,128)(2,1)} async-done(((bf16[3072,384]{1,0:T(8,128)(2,1)}), bf16[3072,768]{1,0:T(8,128)(2,1)}) %all-gather.23.cloned.1.call-update) | async-done | bytes 4718608 | tf_op jit(solution)/shard_map/all_gather | solution.py:183
  419.7 17.9 %convert_reduce_fusion = (f32[3072]{0:T(1024)}, bf16[1032,3072]{1,0:T(8,128)(2,1)}) fusion(f32[1032,3072]{1,0:T(8,128)} %get-tuple-element.91, f32[1032,3072]{1,0:T(8,128)} %get-tuple-element.112, bf16[1032,768]{1,0:T(8,128)(2,1)S(1)} %copy-done.15, bf16[3072,768]{1,0:T(8,128)(2,1)} %all-gather.23.cloned.1.call-done), kind=kOutput, calls=%fused_computation.22 | convolution fusion | flops 4920308736 | bytes 38019072 | tf_op jit(solution)/shard_map/dot_general | solution.py:31
  467.6 22.6 %fusion.44 = bf16[12,64,1032]{2,1,0:T(8,128)(2,1)} fusion(bf16[1032,12,64]{0,2,1:T(8,128)(2,1)} %bitcast.92, f32[12,1032,1032]{1,2,0:T(8,128)} %get-tuple-element.109, f32[12,1032]{1,0:T(8,128)S(1)} %copy-done.59), kind=kOutput, calls=%fused_computation.68 | convolution fusion | flops 1662230016 | bytes 54340992 | tf_op jit(solution)/shard_map/hqk,qhd->khd/dot_general | solution.py:240
  490.2 22.3 %fusion.110 = f32[12,1032,1032]{1,2,0:T(8,128)} fusion(bf16[1032,12,64]{0,2,1:T(8,128)(2,1)} %bitcast.93, bf16[1032,12,64]{0,2,1:T(8,128)(2,1)S(1)} %bitcast.91), kind=kOutput, calls=%fused_computation.214 | convolution fusion | flops 1635876864 | bytes 54291456 | tf_op jit(solution)/shard_map/qhd,khd->hqk/dot_general | solution.py:241
  515.0 71.9 %fusion.37 = bf16[12,64,1032]{2,1,0:T(8,128)(2,1)} fusion(bf16[1032,12,64]{0,2,1:T(8,128)(2,1)} %bitcast.100, f32[12,1032,1032]{1,2,0:T(8,128)} %fusion.110, pred[1032,1032]{0,1:T(8,128)(4,1)} %broadcast_compare_fusion, f32[12,1032,1032]{1,2,0:T(8,128)} %get-tuple-element.109, f32[12,1032]{1,0:T(8,128)S(1)} %copy-done.59), kind=kOutput, calls=%fused_computation.64 | convolution fusion | flops 1726937472 | bytes 106527168 | tf_op jit(solution)/shard_map/hqk,khd->qhd/dot_general | solution.py:244
  586.9 73.9 %fusion.34 = bf16[12,64,1032]{2,1,0:T(8,128)(2,1)} fusion(bf16[1032,12,64]{0,2,1:T(8,128)(2,1)S(1)} %bitcast.98, f32[12,1032,1032]{1,2,0:T(8,128)} %fusion.110, pred[1032,1032]{0,1:T(8,128)(4,1)} %broadcast_compare_fusion, f32[12,1032,1032]{1,2,0:T(8,128)} %get-tuple-element.109, f32[12,1032]{1,0:T(8,128)} %get-tuple-element.108), kind=kOutput, calls=%fused_computation.63 | convolution fusion | flops 1726937472 | bytes 106527168 | tf_op jit(solution)/shard_map/hqk,qhd->khd/dot_general | solution.py:247
  805.6 44.4 %reduce-scatter.23.cloned.1.call-done = bf16[768,1536]{1,0:T(8,128)(2,1)} async-done(((bf16[768,3072]{1,0:T(8,128)(2,1)}), bf16[768,1536]{1,0:T(8,128)(2,1)}) %reduce-scatter.23.cloned.1.call-update) | async-done | bytes 2359312 | tf_op jit(solution)/shard_map/reduce_scatter | solution.py:305
  866.6 33.7 %all-reduce.2 = bf16[3072]{0:T(1024)(128)(2,1)S(1)} all-reduce(bf16[3072]{0:T(1024)(128)(2,1)S(1)} %get-tuple-element.87), channel_id=12, replica_groups=mesh['dp'=16,'fsdp'=2] {'dp'}, use_global_device_ids=true, to_apply=%region_41.42.clone | all-reduce | flops 3072 | bytes 12288
  909.1 56.4 %reduce-scatter.21.cloned.1.call-done = bf16[48,384]{1,0:T(8,128)(2,1)} async-done(((bf16[768,384]{1,0:T(8,128)(2,1)}), bf16[48,384]{1,0:T(8,128)(2,1)}) %reduce-scatter.21.cloned.1.call-update) | async-done | bytes 36880 | tf_op jit(solution)/shard_map/reduce_scatter | solution.py:317
  966.9 255.0 %all-reduce.10.cloned.1.call-done = f32[70,49920]{1,0:T(8,128)} async-done(((f32[70,49920]{1,0:T(8,128)}), f32[70,49920]{1,0:T(8,128)}) %all-reduce.10.cloned.1.call-update) | async-done | bytes 13977616
  1227.6 40.9 %all-reduce.3 = (f32[128]{0:T(128)}, f32[9,768]{1,0:T(8,128)}) all-reduce(f32[128]{0:T(128)S(1)} %get-tuple-element.113, f32[9,768]{1,0:T(8,128)S(1)} %pad_maximum_fusion.4), channel_id=1, replica_groups=mesh['dp'=16,'fsdp'=2] {'dp','fsdp'}, use_global_device_ids=true, to_apply=%region_20.21 | all-reduce | flops 7040 | bytes 56320 | tf_op jit(solution)/shard_map/psum | solution.py:295
  1268.6 17.6 %reduce-scatter.19.cloned.1.call-done = bf16[48,1152]{1,0:T(8,128)(2,1)} async-done(((bf16[768,1152]{1,0:T(8,128)(2,1)}), bf16[48,1152]{1,0:T(8,128)(2,1)}) %reduce-scatter.19.cloned.1.call-update) | async-done | bytes 110608 | tf_op jit(solution)/shard_map/reduce_scatter | solution.py:314
  1287.7 64.4 %reduce-scatter.27.cloned.1.call-done = bf16[192,384]{1,0:T(8,128)(2,1)} async-done(((bf16[3072,384]{1,0:T(8,128)(2,1)}), bf16[192,384]{1,0:T(8,128)(2,1)}) %reduce-scatter.27.cloned.1.call-update) | async-done | bytes 147472 | tf_op jit(solution)/shard_map/reduce_scatter | solution.py:323
  1353.8 64.0 %reduce-scatter.25.cloned.1.call-done = bf16[48,1536]{1,0:T(8,128)(2,1)} async-done(((bf16[768,1536]{1,0:T(8,128)(2,1)}), bf16[48,1536]{1,0:T(8,128)(2,1)}) %reduce-scatter.25.cloned.1.call-update) | async-done | bytes 147472 | tf_op jit(solution)/shard_map/reduce_scatter | solution.py:320
  1419.5 122.0 %all-reduce.8.cloned.1.call-done = f32[128,128]{1,0:T(8,128)} async-done(((f32[128,128]{1,0:T(8,128)}), f32[128,128]{1,0:T(8,128)}) %all-reduce.8.cloned.1.call-update) | async-done | bytes 65552 | tf_op jit(solution)/shard_map/psum | solution.py:295
  (290 shorter events, 325.6 us)
Async XLA Ops:
  7.2 235.5 %copy-start = (bf16[1024,640]{1,0:T(8,128)(2,1)S(1)}, bf16[1024,640]{1,0:T(8,128)(2,1)}, u32[]{:S(2)}) copy-start(bf16[1024,640]{1,0:T(8,128)(2,1)} %param.19) | copy-start | bytes 3932164
  7.2 46.1 %all-gather.11.cloned.1.call-start = ((), (), s32[]{:S(2)}) async-start(), calls=%async_computation.9 | async-start | bytes 1880064 | tf_op jit(solution)/shard_map/all_gather | solution.py:172
  7.9 89.3 %all-gather.17.cloned.1.call-start = ((), (), s32[]{:S(2)}) async-start(), calls=%async_computation.12 | async-start | bytes 2506752 | tf_op jit(solution)/shard_map/all_gather | solution.py:174
  8.8 156.9 %all-gather.21.cloned.1.call-start = ((), (), s32[]{:S(2)}) async-start(), calls=%async_computation.14 | async-start | bytes 2506752 | tf_op jit(solution)/shard_map/all_gather | solution.py:175
  9.5 208.2 %all-gather.25.cloned.1.call-start = ((), (), s32[]{:S(2)}) async-start(), calls=%async_computation.22 | async-start | bytes 7907328 | tf_op jit(solution)/shard_map/all_gather | solution.py:148
  16.4 250.6 %all-gather.13.cloned.1.call-start = ((), (), s32[]{:S(2)}) async-start(), calls=%async_computation.10 | async-start | bytes 5308416 | tf_op jit(solution)/shard_map/all_gather | solution.py:180
  53.3 282.2 %all-gather.15.cloned.1.call-start = ((), (), s32[]{:S(2)}) async-start(), calls=%async_computation.11 | async-start | bytes 1769472 | tf_op jit(solution)/shard_map/all_gather | solution.py:181
  75.9 279.6 %all-gather.19.cloned.1.call-start = ((), (), s32[]{:S(2)}) async-start(), calls=%async_computation.13 | async-start | bytes 7077888 | tf_op jit(solution)/shard_map/all_gather | solution.py:182
  97.2 322.5 %all-gather.23.cloned.1.call-start = ((), (), s32[]{:S(2)}) async-start(), calls=%async_computation.15 | async-start | bytes 7077888 | tf_op jit(solution)/shard_map/all_gather | solution.py:183
  156.8 301.4 %copy-start.31 = (f32[768]{0:T(1024)}, f32[768]{0:T(1024)S(1)}, u32[]{:S(2)}) copy-start(f32[768]{0:T(1024)S(1)} %get-tuple-element.80) | copy-start | bytes 9220
  165.7 617.5 %reduce-scatter.31.cloned.1.call-start = ((), (), s32[]{:S(2)}) async-start(), calls=%async_computation.24 | async-start | bytes 1769472
  514.9 282.3 %reduce-scatter.29.cloned.1.call-start = ((), (), s32[]{:S(2)}) async-start(), calls=%async_computation.23 | async-start | bytes 5308416
  676.8 124.4 %reduce-scatter.33.cloned.1.call-start = ((), (), s32[]{:S(2)}) async-start(), calls=%async_computation.25 | async-start | bytes 7077888
  696.4 153.6 %reduce-scatter.23.cloned.1.call-start = ((), (), s32[]{:S(2)}) async-start(), calls=%async_computation.19 | async-start | bytes 7077888 | tf_op jit(solution)/shard_map/reduce_scatter | solution.py:305
  748.9 158.8 %reduce-scatter.35.cloned.1.call-start = ((), (), s32[]{:S(2)}) async-start(), calls=%async_computation.26 | async-start | bytes 208896
  752.0 213.5 %reduce-scatter.21.cloned.1.call-start = ((), (), s32[]{:S(2)}) async-start(), calls=%async_computation.18 | async-start | bytes 626688 | tf_op jit(solution)/shard_map/reduce_scatter | solution.py:317
  785.4 436.5 %all-reduce.10.cloned.1.call-start = ((), (), s32[]{:S(2)}) async-start(), calls=%async_computation.27 | async-start | bytes 28753920
  797.1 489.0 %reduce-scatter.19.cloned.1.call-start = ((), (), s32[]{:S(2)}) async-start(), calls=%async_computation.17 | async-start | bytes 1880064 | tf_op jit(solution)/shard_map/reduce_scatter | solution.py:314
  801.1 551.0 %reduce-scatter.27.cloned.1.call-start = ((), (), s32[]{:S(2)}) async-start(), calls=%async_computation.21 | async-start | bytes 2506752 | tf_op jit(solution)/shard_map/reduce_scatter | solution.py:323
  805.5 612.3 %reduce-scatter.25.cloned.1.call-start = ((), (), s32[]{:S(2)}) async-start(), calls=%async_computation.20 | async-start | bytes 2506752 | tf_op jit(solution)/shard_map/reduce_scatter | solution.py:320
  850.0 691.4 %all-reduce.8.cloned.1.call-start = ((), (), s32[]{:S(2)}) async-start(), calls=%async_computation.16 | async-start | bytes 131072 | tf_op jit(solution)/shard_map/psum | solution.py:295
  901.1 320.7 %copy-start.22 = (f32[70,128]{1,0:T(8,128)S(1)}, f32[70,128]{1,0:T(8,128)}, u32[]{:S(2)}) copy-start(f32[70,128]{1,0:T(8,128)} %copy-done.21) | copy-start | bytes 107524
  901.1 322.4 %copy-start.18 = (f32[70,64]{1,0:T(8,128)S(1)}, f32[70,64]{1,0:T(8,128)}, u32[]{:S(2)}) copy-start(f32[70,64]{1,0:T(8,128)} %copy-done.17) | copy-start | bytes 53764
  901.2 322.4 %copy-start.20 = (f32[70,64]{1,0:T(8,128)S(1)}, f32[70,64]{1,0:T(8,128)}, u32[]{:S(2)}) copy-start(f32[70,64]{1,0:T(8,128)} %copy-done.19) | copy-start | bytes 53764
  (56 other events, 2859.2 us)
Sparse Core Ops, SparseCore 0:
  10.2 43.0 all-gather.10
  55.6 41.5 all-gather.16
  99.5 41.1 all-gather.20
  144.0 73.6 all-gather.24
  219.1 47.9 all-gather.12
  268.4 22.7 all-gather.14
  292.8 62.6 all-gather.18
  357.0 62.6 all-gather.22
  515.0 21.7 reduce-scatter.30
  676.9 48.5 reduce-scatter.28
  727.8 59.8 reduce-scatter.32
  789.9 60.0 reduce-scatter.22
  854.1 53.5 reduce-scatter.34
  911.7 53.7 reduce-scatter.20
  972.8 249.0 all-reduce.9
  1226.0 60.1 reduce-scatter.18
  1290.2 61.8 reduce-scatter.26
  1355.8 62.0 reduce-scatter.24
  1424.9 116.5 all-reduce.7
where the time goes:
time: 1560 us; the launch traced here: 1550 us
  waiting for transfers between devices  795 us (51%)
  matrix products  399 us (26%)
  blocking collectives  155 us (10%)
  local copies, waits for them, and re-layouts  124 us (8%)
  other arithmetic  57.3 us (4%)
  between operations  18.4 us (1%)
    unnamed x24, waiting for transfers between devices  260 us
    psum x1, waiting for transfers between devices, body(): lax.psum((meta_part, gen_in_part, gen_bias_part), ('dp', 'fsdp'))  122 us
    dot_general x1, matrix products, body(): jnp.einsum('hqk,qhd->khd', d_scores, query, preferred_element_type=jnp.fl...  73.9 us
    dot_general x1, matrix products, body(): jnp.einsum('hqk,khd->qhd', d_scores, keys, preferred_element_type=jnp.flo...  71.9 us
    unnamed x2, blocking collectives  66.3 us
    reduce_scatter x1, waiting for transfers between devices, body(): lax.psum_scatter(down_cols.astype(jnp.bfloat16), 'dp', scatter_dimension=...  64.4 us
    reduce_scatter x1, waiting for transfers between devices, body(): lax.psum_scatter(up_cols.astype(jnp.bfloat16), 'dp', scatter_dimension=0,...  64 us
    reduce_scatter x1, waiting for transfers between devices, body(): lax.psum_scatter(out_cols.astype(jnp.bfloat16), 'dp', scatter_dimension=0...  56.4 us
  transfers between devices with their start and end apart: 19, of which 14 were waited for; matrix products, arithmetic and copies ran while one was open for 31% of the time, Pallas kernels for 0%

commit v1 on v0

--- a/solution.py
+++ b/solution.py
@@ -3,6 +3,8 @@
 import jax
 import jax.numpy as jnp
 from jax import lax
+from jax.experimental import pallas as pl
+from jax.experimental.pallas import tpu as pltpu
 from jax.sharding import PartitionSpec as P
 
 D = 768
@@ -111,7 +113,7 @@
     return (scale * inside, gain_grad, shift_grad)
 
 
-def body(
+def body_general(
     pixels,
     wave_table,
     band_count,
@@ -346,7 +348,1260 @@
     )
 
 
+LIVE = 1032
+ROWS = 1040
+TILE = 208
+TILES = 5
+NZ = 4
+GROUPS = 16
+PIECE = 144
+COVER = 14
+VMEM_ASK = 60 * 1024 * 1024
+BF = jnp.bfloat16
+F32 = jnp.float32
+
+
+def nt_dot(left, right):
+    return lax.dot_general(left, right, (((1,), (1,)), ((), ())), preferred_element_type=F32)
+
+
+def nn_dot(left, right):
+    return lax.dot_general(left, right, (((1,), (0,)), ((), ())), preferred_element_type=F32)
+
+
+def spot():
+    group = lax.axis_index("dp")
+    return group // 4, (group // 2) % 2, group % 2, lax.axis_index("fsdp")
+
+
+def device(z, y, c, x):
+    return {"dp": z * 4 + y * 2 + c, "fsdp": x}
+
+
+def remote(source, target, sems, slot, where):
+    return pltpu.make_async_remote_copy(
+        src_ref=source,
+        dst_ref=target,
+        send_sem=sems[0].at[slot],
+        recv_sem=sems[1].at[slot],
+        device_id=where,
+        device_id_type=pl.DeviceIdType.MESH,
+    )
+
+
+def greet(others):
+    barrier = pltpu.get_barrier_semaphore()
+    for where in others:
+        pl.semaphore_signal(
+            barrier, inc=1, device_id=where, device_id_type=pl.DeviceIdType.MESH
+        )
+    pl.semaphore_wait(barrier, len(others))
+
+
+def columns(ref, x):
+    width = ref.shape[-1] // 2
+    return pl.ds(pl.multiple_of(x * width, 128), width)
+
+
+def group_peers(z, y, c, x):
+    return [
+        ((dz, dy, dc), device((z + dz) % NZ, (y + dy) % 2, (c + dc) % 2, x))
+        for dz in range(NZ)
+        for dy in range(2)
+        for dc in range(2)
+        if dz + dy + dc
+    ]
+
+
+def first_hop(shard, whole, sems, first, local, here):
+    z, y, c, x = here
+    target = whole.at[z, y, c, :, columns(whole, x)]
+    return pltpu.make_async_copy(shard, target, local), [
+        remote(shard, target, sems, first + k - 1, device((z + k) % NZ, y, c, x))
+        for k in range(1, NZ)
+    ]
+
+
+CHUNK = 768
+BANDS = ((0, 256), (256, 256), (512, 256), (768, 256), (1024, 8))
+
+
+def gelu_parts(values):
+    bell = jnp.exp(values * values * (-0.5))
+    step = 1.0 / (1.0 + (0.3275911 * math.sqrt(0.5)) * jnp.abs(values))
+    poly = 0.5 * 1.061405429 * step - 0.5 * 1.453152027
+    poly = poly * step + 0.5 * 1.421413741
+    poly = poly * step - 0.5 * 0.284496736
+    poly = poly * step + 0.5 * 0.254829592
+    tail = poly * step * bell
+    below = jnp.where(values < 0.0, tail, 1.0 - tail)
+    return values * below, below + values * bell * (1.0 / math.sqrt(2.0 * math.pi))
+
+
+def standard(values):
+    centred = values - jnp.mean(values, axis=-1, keepdims=True)
+    scale = lax.rsqrt(jnp.mean(centred * centred, axis=-1, keepdims=True) + 1e-05)
+    return centred * scale, scale
+
+
+def column_sum(values):
+    return jnp.sum(values, axis=0, keepdims=True)
+
+
+def put_rows(target, first, count, values):
+    if count % 16:
+        values = jnp.concatenate(
+            [values, jnp.zeros((16 - count % 16, values.shape[1]), values.dtype)], axis=0
+        )
+    target[first : first + values.shape[0], :] = values
+
+
+class Gather:
+    def __init__(self, whole, sems, first, here):
+        z, y, c, x = here
+        mine, other = columns(whole, x), columns(whole, 1 - x)
+        block = whole.at[:, y, c, :, mine]
+        from_x = whole.at[:, y, c, :, other]
+        from_y = whole.at[:, 1 - y, c, :, mine]
+        far_low = whole.at[0:2, 1 - y, c, :, other]
+        far_high = whole.at[2:4, 1 - y, c, :, other]
+        across, beside, twin = device(z, y, c, 1 - x), device(z, 1 - y, c, x), device(z, y, 1 - c, x)
+        self.to_x = remote(block, block, sems, first, across)
+        self.to_y = remote(block, block, sems, first + 1, beside)
+        self.core = [remote(block, block, sems, first + 2, twin)]
+        low = whole.at[0:2, y, c, :, other]
+        high = whole.at[2:4, 1 - y, c, :, mine]
+        self.far_y = remote(low, low, sems, first + 3, beside)
+        self.far_x = remote(high, high, sems, first + 4, across)
+        for step, part in enumerate((from_x, from_y, far_low, far_high)):
+            self.core.append(remote(part, part, sems, first + 5 + step, twin))
+
+    def stage_b(self):
+        self.to_x.start()
+        self.to_y.start()
+        self.core[0].start()
+
+    def stage_c(self, receive=True):
+        if receive:
+            self.to_x.wait_recv()
+        self.far_y.start()
+        self.core[1].start()
+        if receive:
+            self.to_y.wait_recv()
+        self.far_x.start()
+        self.core[2].start()
+
+    def stage_d(self):
+        self.far_y.wait_recv()
+        self.core[3].start()
+        self.far_x.wait_recv()
+        self.core[4].start()
+
+    def finish(self, receive=True, began=True):
+        skip = 0 if began else 1
+        if receive:
+            for copy in self.core[skip:]:
+                copy.wait_recv()
+        if began:
+            self.to_x.wait_send()
+            self.to_y.wait_send()
+        for copy in (self.far_y, self.far_x, *self.core[skip:]):
+            copy.wait_send()
+
+
+def open_kernel(
+    wq, wo, wu, wd, small, made, pixels, table, places, meta, bands,
+    full_q, full_o, full_u, full_d, params, kernel, tokens, first, qkv,
+    taken, full_small, flat, wide,
+    a_send, a_recv, b_send, b_recv, local_sem, s_send, s_recv, g_send, g_recv,
+):
+    here = z, y, c, x = spot()
+    peers = group_peers(z, y, c, x)
+    across = device(z, y, c, 1 - x)
+    greet([where for _, where in peers] + [across])
+    pairs = ((wq, full_q), (wo, full_o), (wu, full_u), (wd, full_d))
+    hops = [
+        first_hop(shard, whole, (a_send, a_recv), 3 * step, local_sem.at[step], here)
+        for step, (shard, whole) in enumerate(pairs)
+    ]
+    q, o, u = [
+        Gather(whole, (b_send, b_recv), 9 * step, here) for step, (_, whole) in enumerate(pairs[:3])
+    ]
+
+    def start_hop(local, along):
+        local.start()
+        for copy in along:
+            copy.start()
+
+    def end_hop(local, along):
+        local.wait()
+        for copy in along:
+            copy.wait_recv()
+
+    s_sems = (s_send, s_recv)
+    g_sems = (g_send, g_recv)
+    own_made = pltpu.make_async_copy(
+        made.at[z, y, c], taken.at[z, y, c, x], local_sem.at[4]
+    )
+    own_made.start()
+    sends = {}
+    for (dz, dy, dc), where in peers:
+        copy = remote(
+            made.at[(z + dz) % NZ, (y + dy) % 2, (c + dc) % 2],
+            taken.at[z, y, c, x],
+            g_sems,
+            dz * 4 + dy * 2 + dc,
+            where,
+        )
+        copy.start()
+        sends[dz, dy, dc] = copy
+    start_hop(*hops[0])
+    own_small = pltpu.make_async_copy(small, full_small.at[z, y, c], local_sem.at[5])
+    own_small.start()
+    small_z = [
+        remote(small, full_small.at[z, y, c], s_sems, k - 1, device((z + k) % NZ, y, c, x))
+        for k in range(1, NZ)
+    ]
+    for copy in small_z:
+        copy.start()
+    for hop in hops[1:]:
+        start_hop(*hop)
+    own_made.wait()
+    swaps = []
+    for dz in range(NZ):
+        for dy in range(2):
+            for dc in range(2):
+                if dz + dy + dc:
+                    sends[dz, dy, dc].wait_recv()
+        part = taken.at[(z + NZ - dz) % NZ, :, :, x]
+        swap = remote(part, part, g_sems, 16 + dz, across)
+        swap.start()
+        swaps.append(swap)
+    end_hop(*hops[0])
+    q.stage_b()
+    own_small.wait()
+    for copy in small_z:
+        copy.wait_recv()
+    part = full_small.at[:, y, c]
+    small_y = remote(part, part, s_sems, 3, device(z, 1 - y, c, x))
+    small_y.start()
+    for swap in swaps:
+        swap.wait_recv()
+    unpack(taken, flat, wide, kernel)
+    end_hop(*hops[1])
+    q.stage_c()
+    o.stage_b()
+    small_y.wait_recv()
+    part = full_small.at[:, :, c]
+    small_c = remote(part, part, s_sems, 4, device(z, y, 1 - c, x))
+    small_c.start()
+    bias = jnp.concatenate(
+        [
+            column_sum(flat[(PIX * 6 + part) * MAXB : (PIX * 6 + part + 1) * MAXB, :])
+            for part in range(6)
+        ],
+        axis=1,
+    ) / bands[0:1, 0:1]
+    for start, count in BANDS[:-1]:
+        band = slice(start, start + count)
+        made_rows = nn_dot(pixels[band, :], kernel[...])
+        spread = [nn_dot(places[band, way * 256 : (way + 1) * 256], table[...]) for way in range(2)]
+        tokens[band, :] = made_rows + bias + jnp.concatenate(spread, axis=1)
+        if start == 256:
+            q.stage_d()
+    small_c.wait_recv()
+    end_hop(*hops[2])
+    o.stage_c()
+    u.stage_b()
+    params[...] = jnp.zeros_like(params)
+    for n in range(GROUPS):
+        params[...] += full_small[n // 4, (n // 2) % 2, n % 2].astype(F32)
+    tokens[TOK_DEV:LIVE, :] = meta[...]
+    for start, count in BANDS:
+        band = slice(start, start + count)
+        normed, _ = standard(tokens[band, :])
+        first[band, :] = (normed * params[0:1, :] + params[1:2, :]).astype(BF)
+    for copy in q.core:
+        copy.wait_recv()
+    for start, count in BANDS:
+        band = slice(start, start + count)
+        for third in range(3):
+            part = slice(third * D, (third + 1) * D)
+            qkv[band, part] = nn_dot(
+                first[band, :], full_q[:, :, :, :, part].reshape(D, D)
+            ).astype(BF)
+    o.stage_d()
+    end_hop(*hops[3])
+    for gather in (q, o):
+        gather.finish(gather is not q)
+    for copy in (u.to_x, u.to_y, u.core[0]):
+        copy.wait()
+    for copy in (*small_z, small_y, small_c, *sends.values(), *swaps):
+        copy.wait_send()
+    for _, along in hops:
+        for copy in along:
+            copy.wait_send()
+
+
+def opening(w_qkv, w_out, w_up, w_down, small, made, pixels, table, places, meta, bands):
+    anywhere = pl.BlockSpec(memory_space=pl.ANY)
+    vmem = pl.BlockSpec(memory_space=pltpu.VMEM)
+    shards = (w_qkv, w_out, w_up, w_down)
+    outs = [
+        jax.ShapeDtypeStruct((NZ, 2, 2, shard.shape[0], 2 * shard.shape[1]), BF) for shard in shards
+    ]
+    outs += [
+        jax.ShapeDtypeStruct((16, D), F32),
+        jax.ShapeDtypeStruct((MAXB * PIX, D), BF),
+        jax.ShapeDtypeStruct((LIVE, D), F32),
+        jax.ShapeDtypeStruct((LIVE, D), BF),
+        jax.ShapeDtypeStruct((LIVE, 3 * D), BF),
+    ]
+    return pl.pallas_call(
+        open_kernel,
+        out_shape=outs,
+        in_specs=[anywhere] * 6 + [vmem] * 5,
+        out_specs=[vmem] + [anywhere] * 3 + [vmem] * 5,
+        scratch_shapes=[
+            pltpu.VMEM((NZ, 2, 2, 2) + made.shape[3:], BF),
+            pltpu.VMEM((NZ, 2, 2, 16, D), BF),
+            pltpu.VMEM((FLAT, 128), F32),
+            pltpu.VMEM((6, MAXB * PIX, 128), F32),
+        ]
+        + [pltpu.SemaphoreType.DMA((count,)) for count in (12, 12, 27, 27, 6, 5, 5, 20, 20)],
+        compiler_params=pltpu.CompilerParams(
+            collective_id=0, has_side_effects=True, vmem_limit_bytes=VMEM_ASK
+        ),
+    )(*shards, small, made, pixels, table, places, meta, bands)
+
+
+class Scatter:
+    def __init__(self, whole, own, came, low, high, side_x, side_y, last, out, sems, first, here):
+        z, y, c, x = here
+        self.here, self.own, self.came, self.out = here, own, came, out
+        self.low, self.high, self.side_x, self.side_y, self.last = low, high, side_x, side_y, last
+        self.mine, self.other = columns(own, x), columns(own, 1 - x)
+        mine, other = self.mine, self.other
+        across, beside, twin = device(z, y, c, 1 - x), device(z, 1 - y, c, x), device(z, y, 1 - c, x)
+        self.local = pltpu.make_async_copy(whole.at[:, :, c], own, sems[2].at[first // 8])
+        self.core = remote(whole.at[:, :, 1 - c], came, sems, first, twin)
+        self.far_y = remote(own.at[0:2, 1 - y, :, other], low, sems, first + 1, beside)
+        self.far_x = remote(own.at[2:4, 1 - y, :, other], high, sems, first + 2, across)
+        self.to_x = remote(own.at[:, y, :, other], side_x, sems, first + 3, across)
+        self.to_y = remote(own.at[:, 1 - y, :, mine], side_y, sems, first + 4, beside)
+        self.along = [
+            remote(
+                own.at[(z + k) % NZ, y, :, mine], last.at[k - 1], sems, first + 4 + k,
+                device((z + k) % NZ, y, c, x),
+            )
+            for k in range(1, NZ)
+        ]
+
+    def stage_a(self):
+        self.local.start()
+        self.core.start()
+
+    def stage_b(self):
+        self.local.wait()
+        self.core.wait_recv()
+        for at_z in range(NZ):
+            for at_y in range(2):
+                self.own[at_z, at_y] = (
+                    self.own[at_z, at_y].astype(F32) + self.came[at_z, at_y].astype(F32)
+                ).astype(BF)
+        self.far_y.start()
+        self.far_x.start()
+
+    def stage_c(self):
+        _, y, _, _ = self.here
+        self.far_y.wait_recv()
+        for k in range(2):
+            self.own[k, y, :, self.other] = (
+                self.own[k, y, :, self.other].astype(F32) + self.low[k].astype(F32)
+            ).astype(BF)
+        self.to_x.start()
+        self.far_x.wait_recv()
+        for k in range(2):
+            self.own[2 + k, 1 - y, :, self.mine] = (
+                self.own[2 + k, 1 - y, :, self.mine].astype(F32) + self.high[k].astype(F32)
+            ).astype(BF)
+        self.to_y.start()
+
+    def stage_d(self):
+        _, y, _, _ = self.here
+        self.to_x.wait_recv()
+        self.to_y.wait_recv()
+        for k in range(NZ):
+            self.own[k, y, :, self.mine] = (
+                self.own[k, y, :, self.mine].astype(F32)
+                + self.side_x[k].astype(F32)
+                + self.side_y[k].astype(F32)
+            ).astype(BF)
+        for copy in self.along:
+            copy.start()
+
+    def stage_e(self):
+        z, y, _, _ = self.here
+        for copy in self.along:
+            copy.wait_recv()
+        self.out[...] = (
+            self.own[z, y, :, self.mine].astype(F32)
+            + self.last[0].astype(F32)
+            + self.last[1].astype(F32)
+            + self.last[2].astype(F32)
+        )
+        for copy in (self.core, self.far_y, self.far_x, self.to_x, self.to_y, *self.along):
+            copy.wait_send()
+
+
+class Total:
+    def __init__(self, source, out, held, came, slots, send_sem, recv_sem, here):
+        z, y, c, x = here
+        sems = (send_sem, recv_sem)
+        self.source, self.held, self.came, self.slots, self.out = source, held, came, slots, out
+        self.z = z
+        where = (device(z, y, 1 - c, x), device(z, y, c, 1 - x), device(z, 1 - y, c, x))
+        self.steps = [
+            remote(source if step == 0 else held.at[step - 1], came.at[step], sems, step, where[step])
+            for step in range(3)
+        ]
+        self.along = [
+            remote(held.at[2], slots.at[z], sems, 2 + k, device((z + k) % NZ, y, c, x))
+            for k in range(1, NZ)
+        ]
+
+    def begin(self):
+        self.steps[0].start()
+
+    def turn(self, step):
+        self.steps[step].wait_recv()
+        before = self.source[...] if step == 0 else self.held[step - 1]
+        self.held[step] = before + self.came[step]
+        if step < 2:
+            self.steps[step + 1].start()
+        else:
+            self.slots[self.z] = self.held[2]
+            for copy in self.along:
+                copy.start()
+
+    def finish(self):
+        for copy in self.along:
+            copy.wait_recv()
+        self.out[...] = self.slots[0] + self.slots[1] + self.slots[2] + self.slots[3]
+        for copy in (*self.steps, *self.along):
+            copy.wait_send()
+
+
+def near(z, y, c, x):
+    return [
+        device(z, y, c, 1 - x),
+        device(z, 1 - y, c, x),
+        device(z, y, 1 - c, x),
+        *[device((z + k) % NZ, y, c, x) for k in range(1, NZ)],
+    ]
+
+
+def scatter_scratch(rows, width):
+    half = width // 2
+    return [
+        pltpu.VMEM((NZ, 2, rows, width), BF),
+        pltpu.VMEM((NZ, 2, rows, width), BF),
+        pltpu.VMEM((2, rows, half), BF),
+        pltpu.VMEM((2, rows, half), BF),
+        pltpu.VMEM((NZ, rows, half), BF),
+        pltpu.VMEM((NZ, rows, half), BF),
+        pltpu.VMEM((3, rows, half), BF),
+    ]
+
+
+def total_scratch(shape):
+    return [
+        pltpu.VMEM((3,) + shape, F32),
+        pltpu.VMEM((3,) + shape, F32),
+        pltpu.VMEM((NZ,) + shape, F32),
+        pltpu.SemaphoreType.DMA((6,)),
+        pltpu.SemaphoreType.DMA((6,)),
+    ]
+
+
+def piece_start(owner):
+    return (owner * (GENOUT // 32)) // 128
+
+
+def make_kernel(hidden, gen_out, pieces, gen_shift, rows, wide):
+    wide[...] = jnp.zeros_like(wide)
+    wide[:, : gen_out.shape[1]] = gen_out[...].astype(F32)
+    owner = lax.axis_index("dp") * 2 + lax.axis_index("fsdp")
+    gen_shift[...] = pltpu.roll(wide[...], (owner * gen_out.shape[1]) % 128, 1).astype(BF)
+    rows[:, COVER * MAXB :, :] = jnp.zeros((GROUPS, PIECE - COVER * MAXB, 128), F32)
+    for at in range(COVER):
+        made = nn_dot(hidden[...], gen_shift[:, at * 128 : (at + 1) * 128])
+        for group in range(GROUPS):
+            rows[group, at * MAXB : (at + 1) * MAXB, :] = made[group * MAXB : (group + 1) * MAXB]
+    pieces[...] = rows[...].astype(BF)
+
+
+def make_pieces(hidden, gen_out):
+    return pl.pallas_call(
+        make_kernel,
+        out_shape=[
+            jax.ShapeDtypeStruct((GROUPS, PIECE, 128), BF),
+            jax.ShapeDtypeStruct((GEN, COVER * 128), BF),
+        ],
+        scratch_shapes=[
+            pltpu.VMEM((GROUPS, PIECE, 128), F32),
+            pltpu.VMEM((GEN, COVER * 128), F32),
+        ],
+        compiler_params=pltpu.CompilerParams(vmem_limit_bytes=VMEM_ASK),
+    )(hidden, gen_out)
+
+
+FLAT = (GENOUT // 128) * MAXB
+
+
+def unpack(taken, flat, wide, kernel):
+    flat[...] = jnp.zeros_like(flat)
+    used = COVER * MAXB
+    for owner in range(32):
+        first = piece_start(owner) * MAXB
+        count = min(used, FLAT - first)
+        piece = taken[owner // 8, (owner // 4) % 2, (owner // 2) % 2, owner % 2]
+        flat[first : first + count, :] += piece.astype(F32)[:count]
+    for pixel in range(PIX):
+        for part in range(6):
+            first = (pixel * 6 + part) * MAXB
+            wide[part, pl.ds(pixel, MAXB, stride=PIX), :] = flat[first : first + MAXB, :]
+    for part in range(6):
+        kernel[:, part * 128 : (part + 1) * 128] = wide[part].astype(BF)
+
+
+def pack(d_kernel, bias, pieces, wide, flat):
+    for part in range(6):
+        wide[part] = d_kernel[:, part * 128 : (part + 1) * 128]
+        first = (PIX * 6 + part) * MAXB
+        flat[first : first + MAXB, :] = bias[0:MAXB, part * 128 : (part + 1) * 128]
+    flat[FLAT:, :] = jnp.zeros((flat.shape[0] - FLAT, 128), F32)
+    for pixel in range(PIX):
+        for part in range(6):
+            first = (pixel * 6 + part) * MAXB
+            flat[first : first + MAXB, :] = wide[part, pl.ds(pixel, MAXB, stride=PIX), :]
+    for owner in range(32):
+        first = piece_start(owner) * MAXB
+        pieces[owner // 8, (owner // 4) % 2, (owner // 2) % 2, owner % 2] = flat[
+            first : first + PIECE, :
+        ].astype(BF)
+
+
+def norm_rows_back(value, upstream, gain):
+    normed, scale = standard(value)
+    scaled = upstream * gain
+    inside = (
+        scaled
+        - jnp.mean(scaled, axis=-1, keepdims=True)
+        - normed * jnp.mean(scaled * normed, axis=-1, keepdims=True)
+    )
+    return scale * inside, column_sum(upstream * normed), column_sum(upstream)
+
+
+def close_kernel(
+    d_qkv, first, w_qkv, tokens, d_after, params, pixels, kernel, meta_mix, late, b_grad, live,
+    hidden, gen_shift, slope, codes,
+    out_grad, in_grad, out_q, out_early, pixel_grad,
+    d_tokens, grad_q, pieces, taken, flat, wide, rows, source, early,
+    send_sem, recv_sem, local_sem, q_send, q_recv, *rest,
+):
+    here = z, y, c, x = spot()
+    peers = [
+        ((dz, dy, dc, dx), ((z + dz) % NZ, (y + dy) % 2, (c + dc) % 2, (x + dx) % 2))
+        for dz in range(NZ)
+        for dy in range(2)
+        for dc in range(2)
+        for dx in range(2)
+        if dz + dy + dc + dx
+    ]
+    greet([device(*where) for _, where in peers])
+    scatter = Scatter(
+        grad_q, *rest[10:17], out_q, (q_send, q_recv, local_sem), 0, here
+    )
+    begin = Total(early, out_early, *rest[0:5], here)
+    for third in range(3):
+        part = slice(third * D, (third + 1) * D)
+        grad_q[:, :, :, :, part] = (
+            inner_dot(first[...], d_qkv[:, part]).astype(BF).reshape(NZ, 2, 2, -1, D)
+        )
+    scatter.stage_a()
+    gain = shift = jnp.zeros((1, D), F32)
+    for start, count in BANDS:
+        band = slice(start, start + count)
+        upstream = nt_dot(d_qkv[band, :], w_qkv[...].reshape(D, 3 * D))
+        d_norm, gain_part, shift_part = norm_rows_back(tokens[band, :], upstream, params[0:1, :])
+        gain += gain_part
+        shift += shift_part
+        d_tokens[band, :] = (d_after[band, :] + d_norm).astype(BF)
+    scatter.stage_b()
+    patches = d_tokens[0:TOK_DEV, :]
+    d_kernel = inner_dot(pixels[...], patches)
+    sums = column_sum(patches.astype(F32))
+    pack(d_kernel, live[...] * sums, pieces, wide, flat)
+    own = pltpu.make_async_copy(pieces.at[z, y, c, x], taken.at[z, y, c, x], local_sem.at[1])
+    own.start()
+    sends = []
+    for (dz, dy, dc, dx), where in peers:
+        copy = remote(
+            pieces.at[where],
+            taken.at[z, y, c, x],
+            (send_sem, recv_sem),
+            dz * 8 + dy * 4 + dc * 2 + dx,
+            device(*where),
+        )
+        copy.start()
+        sends.append(copy)
+    early[0:16, :] = lax.dot_general(
+        meta_mix[...],
+        d_tokens[TOK_DEV:LIVE, :].astype(F32),
+        (((1,), (0,)), ((), ())),
+        precision=lax.Precision.HIGHEST,
+        preferred_element_type=F32,
+    )
+    early[16:24, :] = late[...]
+    early[16:17, :] = gain
+    early[17:18, :] = shift
+    early[24:32, :] = b_grad[...]
+    begin.begin()
+    scatter.stage_c()
+    begin.turn(0)
+    for start, count in BANDS[:-1]:
+        band = slice(start, start + count)
+        pixel_grad[band, :] = nt_dot(d_tokens[band, :], kernel[...])
+    begin.turn(1)
+    scatter.stage_d()
+    begin.turn(2)
+    own.wait()
+    for copy in sends:
+        copy.wait_recv()
+    for n in range(32):
+        block = taken[n // 8, (n // 4) % 2, (n // 2) % 2, n % 2].astype(F32)
+        for at in range(COVER):
+            rows[at, n * MAXB : (n + 1) * MAXB, :] = block[at * MAXB : (at + 1) * MAXB]
+    d_hidden = jnp.zeros((32 * MAXB, GEN), F32)
+    for at in range(COVER):
+        d_hidden += nt_dot(rows[at].astype(BF), gen_shift[:, at * 128 : (at + 1) * 128])
+    d_before = d_hidden * slope[...]
+    source[0:GEN, :] = lax.dot_general(
+        codes[...],
+        d_before,
+        (((1,), (0,)), ((), ())),
+        precision=lax.Precision.HIGHEST,
+        preferred_element_type=F32,
+    )
+    source[GEN : GEN + 8, :] = jnp.broadcast_to(column_sum(d_before), (8, GEN))
+    total = Total(source, in_grad, *rest[5:10], here)
+    total.begin()
+    for at in range(COVER):
+        out_grad[:, at * 128 : (at + 1) * 128] = nn_dot(hidden[...], rows[at].astype(BF))
+    scatter.stage_e()
+    begin.finish()
+    for step in range(3):
+        total.turn(step)
+    total.finish()
+    for copy in sends:
+        copy.wait_send()
+
+
+def closing(
+    d_qkv, first, w_qkv, tokens, d_after, params, pixels, kernel, meta_mix, late, b_grad, live,
+    hidden, gen_shift, slope, codes,
+):
+    vmem = pl.BlockSpec(memory_space=pltpu.VMEM)
+    small, early = (GEN + 8, GEN), (32, D)
+    held = (NZ, 2, 2, 2, PIECE, 128)
+    _, _, _, rows, width = w_qkv.shape
+    return pl.pallas_call(
+        close_kernel,
+        in_specs=[vmem] * 16,
+        out_specs=[vmem] * 5,
+        out_shape=[
+            jax.ShapeDtypeStruct((GEN, COVER * 128), F32),
+            jax.ShapeDtypeStruct(small, F32),
+            jax.ShapeDtypeStruct((rows, width // 2), F32),
+            jax.ShapeDtypeStruct(early, F32),
+            jax.ShapeDtypeStruct(pixels.shape, F32),
+        ],
+        scratch_shapes=[
+            pltpu.VMEM((LIVE, D), BF),
+            pltpu.VMEM(w_qkv.shape, BF),
+            pltpu.VMEM(held, BF),
+            pltpu.VMEM(held, BF),
+            pltpu.VMEM((FLAT + 64, 128), F32),
+            pltpu.VMEM((6, MAXB * PIX, 128), F32),
+            pltpu.VMEM((COVER, 32 * MAXB, 128), F32),
+            pltpu.VMEM(small, F32),
+            pltpu.VMEM(early, F32),
+            pltpu.SemaphoreType.DMA((32,)),
+            pltpu.SemaphoreType.DMA((32,)),
+            pltpu.SemaphoreType.DMA((2,)),
+            pltpu.SemaphoreType.DMA((8,)),
+            pltpu.SemaphoreType.DMA((8,)),
+            *total_scratch(early),
+            *total_scratch(small),
+            *scatter_scratch(rows, width),
+        ],
+        compiler_params=pltpu.CompilerParams(
+            collective_id=2, has_side_effects=True, vmem_limit_bytes=VMEM_ASK
+        ),
+    )(
+        d_qkv, first, w_qkv, tokens, d_after, params, pixels, kernel, meta_mix, late, b_grad, live,
+        hidden, gen_shift, slope, codes,
+    )
+
+
+def mask_lanes(kind):
+    row = lax.broadcasted_iota(jnp.int32, (ROWS, 128), 0)
+    lane = lax.broadcasted_iota(jnp.int32, (ROWS, 128), 1)
+    patch = jnp.where(kind == 1, 0, row // (TOK_DEV // SLOTS))
+    segment = jnp.where(row < TOK_DEV, patch, (row - TOK_DEV) // 2)
+    hot = (lane == segment) & (row < LIVE)
+    for_query = jnp.where(hot, 1.0, 0.0)
+    for_key = jnp.where(
+        lane < SLOTS, jnp.where(hot, 0.0, -1e30), jnp.where(lane < SLOTS + 3, 1.0, 0.0)
+    )
+    return for_query.astype(BF), for_key.astype(BF)
+
+
+def pad_into(target, source):
+    target[0:TOK_DEV, 0:128] = source[0:TOK_DEV, :]
+    target[TOK_DEV:ROWS, 0:128] = jnp.concatenate(
+        [source[TOK_DEV:LIVE, :], jnp.zeros((ROWS - LIVE, 128), BF)], axis=0
+    )
+
+
+def tile_rows(source, first):
+    if first + TILE <= LIVE:
+        return source[first : first + TILE, :]
+    part = source[first:LIVE, :]
+    return jnp.concatenate([part, jnp.zeros((first + TILE - LIVE, 128), part.dtype)], axis=0)
+
+
+def attend_kernel(
+    q_ref, k_ref, v_ref, mask_q, mask_k, _u, _d, mixed, log_sum, full_u, full_d,
+    keys, values, send_sem, recv_sem,
+):
+    step = pl.program_id(0)
+    here = spot()
+    u, d = [
+        Gather(whole, (send_sem, recv_sem), 9 * at, here)
+        for at, whole in enumerate((full_u, full_d))
+    ]
+
+    @pl.when(step == 0)
+    def _():
+        greet(near(*here))
+        u.stage_c(False)
+        d.stage_b()
+
+    @pl.when(step == 3)
+    def _():
+        u.stage_d()
+        d.stage_c()
+
+    lane = lax.broadcasted_iota(jnp.int32, (TILE, 128), 1)
+    pad_into(keys, k_ref)
+    keys[:, 128:256] = mask_k[...]
+    pad_into(values, v_ref)
+    values[:, 128:256] = jnp.ones((ROWS, 128), BF)
+    for tile in range(TILES):
+        first = tile * TILE
+        both = tile_rows(q_ref, first) * BF(0.125)
+        results, sums = [], []
+        for head in range(2):
+            query = jnp.where((lane < HEAD) == (head == 0), both, BF(0))
+            scores = nt_dot(
+                jnp.concatenate([query, mask_q[first : first + TILE, :]], axis=1), keys[...]
+            )
+            peak = jnp.max(scores, axis=1, keepdims=True)
+            expo = jnp.exp(scores - peak).astype(BF)
+            made = nn_dot(expo, values[...])
+            totals = made[:, 128:256]
+            results.append(made[:, 0:128] / totals)
+            sums.append(peak + jnp.log(totals))
+        count = min(TILE, LIVE - first)
+        mixed[first : first + count, :] = jnp.where(lane < HEAD, *results)[:count].astype(BF)
+        log_sum[0, first : first + count, :] = jnp.where(lane < HEAD, *sums)[:count]
+
+    @pl.when(step == HEADS // 2 - 1)
+    def _():
+        d.stage_d()
+        u.finish(True, False)
+        d.finish()
+
+
+def attend(qkv, mask_q, mask_k, wholes):
+    def band(first):
+        return pl.BlockSpec((LIVE, 128), lambda pair: (0, first + pair))
+
+    full = pl.BlockSpec((ROWS, 128), lambda pair: (0, 0))
+    anywhere = pl.BlockSpec(memory_space=pl.ANY)
+    return pl.pallas_call(
+        attend_kernel,
+        grid=(HEADS // 2,),
+        in_specs=[band(0), band(6), band(12), full, full] + [anywhere] * 2,
+        out_specs=[band(0), pl.BlockSpec((1, LIVE, 128), lambda pair: (pair, 0, 0))]
+        + [anywhere] * 2,
+        out_shape=[
+            jax.ShapeDtypeStruct((LIVE, D), BF),
+            jax.ShapeDtypeStruct((HEADS // 2, LIVE, 128), F32),
+            *[jax.ShapeDtypeStruct(whole.shape, BF) for whole in wholes],
+        ],
+        input_output_aliases={5: 2, 6: 3},
+        scratch_shapes=[pltpu.VMEM((ROWS, 256), BF)] * 2 + [pltpu.SemaphoreType.DMA((18,))] * 2,
+        compiler_params=pltpu.CompilerParams(
+            collective_id=1, has_side_effects=True, vmem_limit_bytes=VMEM_ASK
+        ),
+    )(qkv, qkv, qkv, mask_q, mask_k, *wholes)
+
+
+def feed_kernel(
+    tokens, mixed, top, w_out, vectors, w_up, w_down,
+    layer_out, d_after, d_mixed, out_grad, rows, up_grad, down_grad, b_grad,
+    second, second_turned, top_full, after, sum_out, sum_second, active, d_upper, proj,
+):
+    step = pl.program_id(0)
+
+    @pl.when(step == 0)
+    def _():
+        for first, count in BANDS:
+            band = slice(first, first + count)
+            value = tokens[band, :] + (nn_dot(mixed[band, :], w_out[...]) + vectors[2:3, :])
+            after[band, :] = value
+            normed, _ = standard(value)
+            put_rows(
+                second, first, count, (normed * vectors[3:4, :] + vectors[4:5, :]).astype(BF)
+            )
+            put_rows(top_full, first, count, top[band, :])
+        second_turned[...] = second[...].T
+        sum_out[...] = jnp.zeros_like(sum_out)
+        b_grad[...] = jnp.zeros_like(b_grad)
+        sum_second[...] = jnp.zeros_like(sum_second)
+
+    total = jnp.zeros((1, CHUNK), F32)
+    for first, count in BANDS:
+        count = -(-count // 16) * 16
+        band = slice(first, first + count)
+        upper = nn_dot(second[band, :], w_up[...]) + vectors[pl.ds(6 + step, 1), :]
+        made, slope = gelu_parts(upper)
+        made = made.astype(BF)
+        active[band, :] = made
+        back = (nt_dot(top_full[band, :], w_down[...]) * slope).astype(BF)
+        d_upper[band, :] = back
+        total += column_sum(back.astype(F32))
+    b_grad[pl.ds(step, 1), :] = total
+    sum_out[...] += nn_dot(active[...], w_down[...])
+    sum_second[...] += nt_dot(d_upper[...], w_up[...])
+    down_grad[...] = inner_dot(active[...], top_full[...]).astype(BF)
+    up_grad[...] = nn_dot(second_turned[...], d_upper[...]).astype(BF)
+
+    @pl.when(step == pl.num_programs(0) - 1)
+    def _():
+        gain = shift = bias = last = jnp.zeros((1, D), F32)
+        for first, count in BANDS:
+            band = slice(first, first + count)
+            value = after[band, :]
+            layer_out[band, :] = (value + sum_out[band, :] + vectors[5:6, :]).astype(BF)
+            normed, scale = standard(value)
+            upstream = sum_second[band, :]
+            gain += column_sum(upstream * normed)
+            shift += column_sum(upstream)
+            scaled = upstream * vectors[3:4, :]
+            inside = (
+                scaled
+                - jnp.mean(scaled, axis=-1, keepdims=True)
+                - normed * jnp.mean(scaled * normed, axis=-1, keepdims=True)
+            )
+            grad_top = top[band, :].astype(F32)
+            last += column_sum(grad_top)
+            result = grad_top + scale * inside
+            d_after[band, :] = result
+            low = result.astype(BF)
+            bias += column_sum(low.astype(F32))
+            put_rows(proj, first, count, low)
+            d_mixed[band, :] = nt_dot(low, w_out[...]).astype(BF)
+        out_grad[...] = inner_dot(mixed[...], proj[0:LIVE, :]).astype(BF)
+        rows[...] = jnp.concatenate([jnp.zeros((2, D), F32), bias, gain, shift, last, jnp.zeros((2, D), F32)], axis=0)
+
+
+def feed(tokens, mixed, top, w_out, vectors, w_up, w_down):
+    width = w_up.shape[1]
+
+    def whole(*shape):
+        return pl.BlockSpec(shape, lambda step: (0, 0))
+
+    across = pl.BlockSpec((D, CHUNK), lambda step: (0, step))
+    down = pl.BlockSpec((CHUNK, D), lambda step: (step, 0))
+    block = whole(LIVE, D)
+    return pl.pallas_call(
+        feed_kernel,
+        grid=(width // CHUNK,),
+        in_specs=[block, block, block, whole(D, D), whole(16, D), across, down],
+        out_specs=[block, block, block, whole(D, D), whole(8, D), across, down, whole(8, D)],
+        out_shape=[
+            jax.ShapeDtypeStruct((LIVE, D), BF),
+            jax.ShapeDtypeStruct((LIVE, D), F32),
+            jax.ShapeDtypeStruct((LIVE, D), BF),
+            jax.ShapeDtypeStruct((D, D), BF),
+            jax.ShapeDtypeStruct((8, D), F32),
+            jax.ShapeDtypeStruct((D, width), BF),
+            jax.ShapeDtypeStruct((width, D), BF),
+            jax.ShapeDtypeStruct((8, D), F32),
+        ],
+        scratch_shapes=[
+            pltpu.VMEM((ROWS, D), BF),
+            pltpu.VMEM((D, ROWS), BF),
+            pltpu.VMEM((ROWS, D), BF),
+            pltpu.VMEM((LIVE, D), F32),
+            pltpu.VMEM((ROWS, D), F32),
+            pltpu.VMEM((ROWS, D), F32),
+            pltpu.VMEM((ROWS, CHUNK), BF),
+            pltpu.VMEM((ROWS, CHUNK), BF),
+            pltpu.VMEM((ROWS, D), BF),
+        ],
+        compiler_params=pltpu.CompilerParams(vmem_limit_bytes=VMEM_ASK),
+    )(tokens, mixed, top, w_out, vectors, w_up, w_down)
+
+
+def three_parts(exact):
+    high = exact.astype(BF)
+    left = exact - high.astype(F32)
+    middle = left.astype(BF)
+    return high, middle, (left - middle.astype(F32)).astype(BF)
+
+
+def attend_back_kernel(
+    q_ref, k_ref, v_ref, d_mixed, mixed, log_sum, mask_q, mask_k, go, gu, gd,
+    out, out_o, out_u, out_d,
+    keys, values, keys_turned, d_query, d_keys, d_values, send_sem, recv_sem, local_sem, *rest,
+):
+    pair, part = pl.program_id(0), pl.program_id(1)
+    here = spot()
+    o, u, d = [
+        Scatter(
+            whole, *rest[7 * at : 7 * at + 7], result, (send_sem, recv_sem, local_sem), 8 * at, here
+        )
+        for at, (whole, result) in enumerate(((go, out_o), (gu, out_u), (gd, out_d)))
+    ]
+
+    @pl.when((pair == 0) & (part == 0))
+    def _():
+        greet(near(*here))
+        d.stage_a()
+        u.stage_a()
+        o.stage_a()
+
+    @pl.when((pair == 0) & (part == 1))
+    def _():
+        d.stage_b()
+
+    @pl.when((pair == 1) & (part == 1))
+    def _():
+        u.stage_b()
+        d.stage_c()
+
+    @pl.when((pair == 2) & (part == 1))
+    def _():
+        o.stage_b()
+        u.stage_c()
+
+    @pl.when((pair == 3) & (part == 1))
+    def _():
+        d.stage_d()
+        o.stage_c()
+
+    @pl.when((pair == 4) & (part == 1))
+    def _():
+        u.stage_d()
+
+    @pl.when((pair == 5) & (part == 1))
+    def _():
+        d.stage_e()
+        o.stage_d()
+
+    @pl.when((pair == 5) & (part == 2))
+    def _():
+        u.stage_e()
+        o.stage_e()
+
+    lane = lax.broadcasted_iota(jnp.int32, (TILE, 128), 1)
+    sub = lax.broadcasted_iota(jnp.int32, (128, TILE), 0)
+
+    def with_parts(exact, rest):
+        a, b, c = three_parts(exact)
+        return jnp.where(
+            lane == SLOTS,
+            a,
+            jnp.where(lane == SLOTS + 1, b, jnp.where(lane == SLOTS + 2, c, rest)),
+        )
+
+    @pl.when(part == 0)
+    def _():
+        pad_into(keys, k_ref)
+        keys[:, 128:256] = mask_k[...]
+        pad_into(values, v_ref)
+        values[:, 128:256] = mask_k[...]
+        keys_turned[...] = keys[:, 0:128].T
+        d_keys[...] = jnp.zeros_like(d_keys)
+        d_values[...] = jnp.zeros_like(d_values)
+        for tile in range(TILES):
+            first = tile * TILE
+            both = tile_rows(q_ref, first) * BF(0.125)
+            up = tile_rows(d_mixed, first)
+            logs = tile_rows(log_sum.at[0], first)
+            product = up.astype(F32) * tile_rows(mixed, first).astype(F32)
+            marks = mask_q[first : first + TILE, :]
+            turned = []
+            for head in range(2):
+                chosen = (lane < HEAD) == (head == 0)
+                query = jnp.where(chosen, both, BF(0))
+                upstream = jnp.where(chosen, up, BF(0))
+                inside = jnp.sum(jnp.where(chosen, product, 0.0), axis=1, keepdims=True)
+                wide_query = jnp.concatenate(
+                    [query, with_parts(-logs[:, head * HEAD : head * HEAD + 1], marks)], axis=1
+                )
+                wide_up = jnp.concatenate(
+                    [upstream, with_parts(-inside, jnp.zeros_like(marks))], axis=1
+                )
+                prob = jnp.exp(nt_dot(keys[...], wide_query))
+                d_scores = (prob * nt_dot(values[...], wide_up)).astype(BF)
+                d_values[...] += nn_dot(prob.astype(BF), upstream)
+                d_keys[...] += nn_dot(d_scores, query)
+                turned.append(nn_dot(keys_turned[...], d_scores))
+            d_query[first : first + TILE, :] = (
+                (jnp.where(sub < HEAD, *turned) * 0.125).T.astype(BF)
+            )
+        out[...] = d_query[0:LIVE, :]
+
+    @pl.when(part == 1)
+    def _():
+        out[...] = d_keys[0:LIVE, :].astype(BF)
+
+    @pl.when(part == 2)
+    def _():
+        out[...] = d_values[0:LIVE, :].astype(BF)
+
+
+def attend_back(qkv, d_mixed, mixed, log_sum, mask_q, mask_k, grads):
+    def band(first):
+        return pl.BlockSpec((LIVE, 128), lambda pair, part: (0, first + pair))
+
+    full = pl.BlockSpec((ROWS, 128), lambda pair, part: (0, 0))
+    shapes = [grad.shape[3:] for grad in grads]
+    outs = [(rows, width // 2) for rows, width in shapes]
+    return pl.pallas_call(
+        attend_back_kernel,
+        grid=(HEADS // 2, 3),
+        in_specs=[
+            band(0), band(6), band(12), band(0), band(0),
+            pl.BlockSpec((1, LIVE, 128), lambda pair, part: (pair, 0, 0)), full, full,
+        ]
+        + [pl.BlockSpec(memory_space=pl.ANY)] * 3,
+        out_specs=[pl.BlockSpec((LIVE, 128), lambda pair, part: (0, part * 6 + pair))]
+        + [pl.BlockSpec(shape, lambda pair, part: (0, 0)) for shape in outs],
+        out_shape=[
+            jax.ShapeDtypeStruct((LIVE, 3 * D), BF),
+            *[jax.ShapeDtypeStruct(shape, F32) for shape in outs],
+        ],
+        scratch_shapes=[
+            pltpu.VMEM((ROWS, 256), BF),
+            pltpu.VMEM((ROWS, 256), BF),
+            pltpu.VMEM((128, ROWS), BF),
+            pltpu.VMEM((ROWS, 128), BF),
+            pltpu.VMEM((ROWS, 128), F32),
+            pltpu.VMEM((ROWS, 128), F32),
+            pltpu.SemaphoreType.DMA((24,)),
+            pltpu.SemaphoreType.DMA((24,)),
+            pltpu.SemaphoreType.DMA((3,)),
+            *[entry for shape in shapes for entry in scatter_scratch(*shape)],
+        ],
+        compiler_params=pltpu.CompilerParams(
+            collective_id=3, has_side_effects=True, vmem_limit_bytes=VMEM_ASK
+        ),
+    )(qkv, qkv, qkv, d_mixed, mixed, log_sum, mask_q, mask_k, *grads)
+
+
+def place_table(kind, ground):
+    quarter = D // 4
+    entry = jnp.arange(64, dtype=jnp.int32)
+    chip = jnp.where(kind == 1, 0, entry // 16)
+    step = jnp.where(kind == 1, entry, entry % 16).astype(F32)
+    scale = (
+        jnp.sum(
+            jnp.where(
+                chip[:, None] == jnp.arange(SLOTS, dtype=jnp.int32)[None, :], ground[None, :], 0
+            ),
+            axis=1,
+        ).astype(F32)
+        / 10.0
+    )
+    omega = 1.0 / 10000.0 ** (jnp.arange(quarter, dtype=F32) / (quarter - 1))
+    angle = (step * scale)[:, None] * omega[None, :]
+    exact = jnp.concatenate([jnp.sin(angle), jnp.cos(angle)], axis=1)
+    table = jnp.concatenate([*three_parts(exact), jnp.zeros((64, 2 * quarter), BF)], axis=0)
+    index = jnp.arange(TOK_DEV, dtype=jnp.int32)[:, None]
+    lane = jnp.arange(512, dtype=jnp.int32)[None, :]
+    across = jnp.where(kind == 1, index // 32, index // 16)
+    along = jnp.where(kind == 1, index % 32, index // 256 * 16 + index % 16)
+    spots = jnp.where(lane < 256, across, along)
+    hot = (lane % 64 == spots) & (lane % 256 < 192)
+    return table, jnp.where(hot, 1.0, 0.0).astype(BF)
+
+
+def body_block(
+    pixels,
+    wave_table,
+    band_count,
+    wave_index,
+    group_sensor,
+    chip_kind,
+    chip_gsd,
+    time_loc,
+    gen_in,
+    gen_bias,
+    gen_out,
+    meta_weight,
+    w_qkv,
+    w_out,
+    w_up,
+    w_down,
+    vectors,
+    b_up,
+    cotangent,
+):
+    group = lax.axis_index("dp")
+    owner = group * 2 + lax.axis_index("fsdp")
+    is_sensor = group_sensor[:, None] == jnp.arange(SENSORS, dtype=jnp.int32)[None, :]
+    bands_of = jnp.sum(jnp.where(is_sensor, band_count[None, :], 0), axis=1)
+    waves_of = jnp.sum(jnp.where(is_sensor[:, :, None], wave_index[None], 0), axis=1)
+    band_total = jnp.sum(jnp.where(jnp.arange(GROUPS, dtype=jnp.int32) == group, bands_of, 0))
+    live = (jnp.arange(MAXB, dtype=jnp.int32)[None, :] < bands_of[:, None]).reshape(-1, 1)
+    codes = wave_code(table_lookup(waves_of.reshape(-1), wave_table))
+    before = exact_dot(codes, gen_in.astype(F32)) + gen_bias.astype(F32)
+    hidden = jnp.where(live, gelu_exact(before), 0.0).astype(BF)
+    slope = jnp.where(live, gelu_slope(before, jnp.ones_like(before)), 0.0)
+    made, gen_shift = make_pieces(hidden, gen_out)
+    width, rows, up_rows = gen_out.shape[1], vectors.shape[0], b_up.shape[0]
+    lane = jnp.arange(D, dtype=jnp.int32)
+    row = jnp.arange(10, dtype=jnp.int32)[:, None]
+    per_row = D // up_rows
+    small = jnp.where(
+        row < 6,
+        jnp.where(
+            (lane // rows == group)[None, :],
+            jnp.concatenate([jnp.tile(vectors.T, (1, GROUPS)), jnp.zeros((4, D), BF)], axis=0),
+            BF(0),
+        ),
+        jnp.where(
+            (row == 6 + group // per_row) & (lane // up_rows == group % per_row)[None, :],
+            jnp.tile(b_up, per_row)[None, :],
+            BF(0),
+        ),
+    )
+    small = jnp.pad(small, ((0, 6), (0, 0)))
+    kind_one = chip_kind[0]
+    band_float = band_total.astype(F32)
+    table, places = place_table(kind_one, chip_gsd[0])
+    meta_mix = jnp.concatenate(
+        [
+            jnp.stack([jnp.ones((SLOTS,), F32), jnp.zeros((SLOTS,), F32)], axis=1).reshape(1, -1),
+            jnp.stack([jnp.zeros_like(time_loc[0]), time_loc[0]], axis=1).reshape(
+                2 * SLOTS, -1
+            ).T,
+            jnp.zeros((7, 2 * SLOTS), F32),
+        ],
+        axis=0,
+    )
+    meta_rows = exact_dot(
+        meta_mix.T, jnp.pad(meta_weight.astype(F32), ((0, 7), (0, 0)))
+    )
+    full_q, full_o, part_u, part_d, params, kernel, tokens_in, first, qkv = opening(
+        w_qkv,
+        w_out,
+        w_up,
+        w_down,
+        small,
+        made.reshape(NZ, 2, 2, PIECE, 128),
+        pixels,
+        table,
+        places,
+        meta_rows,
+        jnp.broadcast_to(band_float, (8, 128)),
+    )
+    mask_q, mask_k = mask_lanes(kind_one)
+    mixed, log_sum, full_u, full_d = attend(qkv, mask_q, mask_k, [part_u, part_d])
+    w_out_all = full_o.reshape(D, D)
+    w_up_all = full_u.reshape(D, -1)
+    w_down_all = full_d.reshape(-1, D)
+    layer_out, d_after, d_mixed, w_out_grad, late, w_up_grad, w_down_grad, b_grad = feed(
+        tokens_in, mixed, cotangent, w_out_all, params, w_up_all, w_down_all
+    )
+    d_qkv, w_out_out, w_up_out, w_down_out = attend_back(
+        qkv,
+        d_mixed,
+        mixed,
+        log_sum,
+        mask_q,
+        mask_k,
+        [
+            grad.reshape(NZ, 2, 2, -1, grad.shape[1])
+            for grad in (w_out_grad, w_up_grad, w_down_grad)
+        ],
+    )
+
+    def by_block(rows_of):
+        return jnp.broadcast_to(
+            rows_of.reshape(GROUPS, 1, MAXB, GEN), (GROUPS, 2, MAXB, GEN)
+        ).reshape(32 * MAXB, GEN)
+
+    own_live = (jnp.arange(16, dtype=jnp.int32) < band_total)[:, None]
+    gen_out_wide, gen_small, w_qkv_out, summed, pixel_grad = closing(
+        d_qkv,
+        first,
+        full_q,
+        tokens_in,
+        d_after,
+        params,
+        pixels,
+        kernel,
+        meta_mix,
+        late,
+        b_grad,
+        jnp.where(own_live, 1.0 / band_float, 0.0),
+        by_block(hidden).T,
+        gen_shift,
+        by_block(slope),
+        by_block(codes).T,
+    )
+    gen_out_grad = lax.dynamic_slice(gen_out_wide, (0, (owner * width) % 128), (GEN, width))
+    vectors_out = lax.dynamic_slice(summed, (16, group * rows), (6, rows)).T
+    b_up_out = lax.dynamic_slice(
+        summed[24:28].reshape(-1), (group * up_rows,), (up_rows,)
+    )
+    return (
+        layer_out,
+        pixel_grad,
+        gen_small[:GEN],
+        gen_small[GEN],
+        gen_out_grad,
+        summed[:9],
+        w_qkv_out,
+        w_out_out,
+        w_up_out,
+        w_down_out,
+        vectors_out,
+        b_up_out,
+    )
+
+
 def solution(mesh):
+    fits = dict(mesh.shape) == {"dp": 16, "fsdp": 2}
+    body = body_block if fits else body_general
     placed = (
         P(("dp", "fsdp"), None),
         P(),

time: 1560 us -> 401 us (0.26)
  waiting for transfers between devices: 795 us -> 0 us
  matrix products: 399 us -> 1.3 us
  Pallas kernels: 0 us -> 355 us
  blocking collectives: 155 us -> 0 us
  local copies, waits for them, and re-layouts: 124 us -> 21.4 us
  other arithmetic: 57.3 us -> 16.8 us
  between operations: 18.4 us -> 2.6 us
    dot_general x21 -> x0, matrix products: 362 us -> none  [the longest x1 73.9 us: body(): jnp.einsum('hqk,qhd->khd', d_scores, query, preferred_element_type=jnp.fl...]
    pallas_call x0 -> x6, Pallas kernels: none -> 355 us  [the longest x1 87.3 us: closing(): pl.pallas_call(close_kernel, in_specs=[vmem] * 16, out_specs=[vmem] * 5,...]
    unnamed x24 -> x0, waiting for transfers between devices: 260 us -> none
    reduce_scatter x5 -> x0, waiting for transfers between devices: 247 us -> none  [the longest x1 64.4 us: body(): lax.psum_scatter(down_cols.astype(jnp.bfloat16), 'dp', scatter_dimension=...]
    all_gather x8 -> x0, waiting for transfers between devices: 167 us -> none  [the longest x1 51.7 us: body(): all_made = lax.all_gather(shard_made, ('dp', 'fsdp'), axis=1, tiled=True)]
    psum x1 -> x0, waiting for transfers between devices: 122 us -> none  [body(): lax.psum((meta_part, gen_in_part, gen_bias_part), ('dp', 'fsdp'))]
    unnamed x2 -> x0, blocking collectives: 66.3 us -> none
    psum x2 -> x0, blocking collectives: 48.9 us -> none  [the longest x1 40.9 us: body(): lax.psum((meta_part, gen_in_part, gen_bias_part), ('dp', 'fsdp'))]
  transfers between devices with their start and end apart: 19 -> 0, of which waited for: 14 -> 0; matrix products, arithmetic and copies ran while one was open for 31% -> 0% of each run, Pallas kernels for 0% -> 0%
where the time goes in v1:
time: 401 us; the launch traced here: 397 us
  Pallas kernels  355 us (89%)
  local copies, waits for them, and re-layouts  21.4 us (5%)
  other arithmetic  16.8 us (4%)
    pallas_call x1, Pallas kernels, closing(): pl.pallas_call(close_kernel, in_specs=[vmem] * 16, out_specs=[vmem] * 5,...  87.3 us
    pallas_call x1, Pallas kernels, opening(): pl.pallas_call(open_kernel, out_shape=outs, in_specs=[anywhere] * 6 + [vm...  82.2 us
    pallas_call x1, Pallas kernels, attend_back(): pl.pallas_call(attend_back_kernel, grid=(HEADS // 2, 3), in_specs=[band(0...  74.4 us
    pallas_call x1, Pallas kernels, feed(): pl.pallas_call(feed_kernel, grid=(width // CHUNK,), in_specs=[block, bloc...  55.7 us
    pallas_call x1, Pallas kernels, attend(): pl.pallas_call(attend_kernel, grid=(HEADS // 2,), in_specs=[band(0), band...  53.1 us

profile of v1, /device:TPU:0, one launch (start us, length us, event | category | flops | bytes accessed | tf_op | source)
XLA Modules:
  0.0 397.5 jit_solution(5748285347598029984)
XLA Ops:
  5.0 0.8 maximum_maximum_fusion.table
  5.8 0.8 copy.51
  8.7 0.8 select_reduce_fusion.2
  11.4 1.0 copy.53.gen_out
  12.4 2.5 shard_map.274
  14.9 1.8 select_convert_fusion.places
  18.8 0.9 fusion.14.meta
  19.7 82.2 %shard_map.275 = (bf16[4,2,2,48,2304]{4,3,2,1,0:T(8,128)(2,1)}, bf16[4,2,2,48,768]{4,3,2,1,0:T(8,128)(2,1)}, bf16[4,2,2,48,3072]{4,3,2,1,0:T(8,128)(2,1)}, bf16[...) custom-call(bf16[48,1152]{1,0:T(8,128)(2,1)} %wq.1, ...), custom_call_target="tpu_custom_call" | custom-call | tf_op jit(solution)/shard_map/pallas_call | solution.py:660
  102.0 2.8 select_convert_fusion.1.mask_k
  104.8 2.8 select_convert_fusion.2.mask_q
  107.5 53.1 %shard_map.276 = (bf16[1032,768]{1,0:T(8,128)(2,1)}, f32[6,1032,128]{2,1,0:T(8,128)}, bf16[4,2,2,48,3072]{4,3,2,1,0:T(8,128)(2,1)}, bf16[4,2,2,192,768]{4,3,2,1,0:T(8,128)(2,1)}) custom-call(bf16[1032,2304]{1,0:T(8,128)(2,1)} %get-tuple-element.46.q_ref.k_ref.v_ref, ...), custom_call_target="tpu_custom_call", output_to_operand_aliasing={{2}: (5, {}), {3}: (6, {})} | custom-call | tf_op jit(solution)/shard_map/pallas_call | solution.py:1144
  160.7 55.7 %shard_map.277 = (bf16[1032,768]{1,0:T(8,128)(2,1)}, f32[1032,768]{1,0:T(8,128)}, bf16[1032,768]{1,0:T(8,128)(2,1)}, bf16[768,768]{1,0:T(8,128)(2,1)}, f32[8,768...) custom-call(f32[1032,768]{1,0:T(8,128)} %get-tuple-element.45.tokens, ...), custom_call_target="tpu_custom_call" | custom-call | tf_op jit(solution)/shard_map/pallas_call | solution.py:1241
  216.4 74.4 %shard_map.278 = (bf16[1032,2304]{1,0:T(8,128)(2,1)}, f32[48,384]{1,0:T(8,128)}, f32[48,1536]{1,0:T(8,128)}, f32[192,384]{1,0:T(8,128)}) custom-call(bf16[1032,2304]{1,0:T(8,128)(2,1)} %get-tuple-element.46.q_ref.k_ref.v_ref, bf16[1032,2304]{1,0:T(8,128)(2,1)} %get-tuple-element.46.q_ref.k_ref.v_ref, bf16[1032,2304]{1,0:T(8,128)(2,1)} %get-tuple-element.46.q_ref.k_ref.v_ref, ...), custom_call_target="tpu_custom_call" | custom-call | tf_op jit(solution)/shard_map/pallas_call | solution.py:1397
  290.9 0.8 copy.56
  291.7 1.3 fusion.25.live
  294.5 0.8 copy.57
  296.0 87.3 %shard_map.279 = (f32[128,1792]{1,0:T(8,128)}, f32[136,128]{1,0:T(8,128)}, f32[48,1152]{1,0:T(8,128)}, f32[32,768]{1,0:T(8,128)}, f32[1024,640]{1,0:T(8,128)}) custom-call(bf16[1032,2304]{1,0:T(8,128)(2,1)} %get-tuple-element.60.d_qkv, bf16[1032,768]{1,0:T(8,128)(2,1)} %get-tuple-element.61.first, bf16[4,2,2,48,2304]{4,3,2,1,0:T(8,128)(2,1)} %get-tuple-element.62.w_qkv, ...), custom_call_target="tpu_custom_call" | custom-call | tf_op jit(solution)/shard_map/pallas_call | solution.py:1019
  383.3 1.6 constant_dynamic-slice_fusion
  385.0 1.2 copy.58
  386.1 1.5 slice.12
  387.6 1.4 slice.14
  390.4 1.4 dynamic-slice_bitcast_fusion
  391.8 1.2 slice_bitcast_fusion
  393.0 1.5 copy.68
  (88 shorter events, 15.5 us)
Async XLA Ops:
  0.6 9.6 %copy-start = (bf16[128,128]{1,0:T(8,128)(2,1)S(1)}, bf16[128,128]{1,0:T(8,128)(2,1)}, u32[]{:S(2)}) copy-start(bf16[128,128]{1,0:T(8,128)(2,1)} %param.27) | copy-start | bytes 98308
  0.7 10.7 %copy-start.3 = (bf16[128,1560]{0,1:T(8,128)(2,1)S(1)}, bf16[128,1560]{0,1:T(8,128)(2,1)}, u32[]{:S(2)}) copy-start(bf16[128,1560]{0,1:T(8,128)(2,1)} %param.29) | copy-start | bytes 1198084
  10.3 8.4 %copy-start.9 = (f32[1,4,8]{2,1,0:T(4,128)S(1)}, f32[1,4,8]{2,1,0:T(4,128)}, u32[]{:S(2)}) copy-start(f32[1,4,8]{2,1,0:T(4,128)} %param.26) | copy-start | bytes 388
  10.3 8.5 %copy-start.10 = (f32[1,8]{1,0:T(1,128)S(1)}, f32[1,8]{1,0:T(1,128)}, u32[]{:S(2)}) copy-start(f32[1,8]{1,0:T(1,128)} %constant.296.clone.1) | copy-start | bytes 100
  10.3 8.5 %copy-start.11 = (bf16[9,768]{1,0:T(8,128)(2,1)S(1)}, bf16[9,768]{1,0:T(8,128)(2,1)}, u32[]{:S(2)}) copy-start(bf16[9,768]{1,0:T(8,128)(2,1)} %param.30) | copy-start | bytes 41476
  216.4 74.4 %copy-start.4 = (bf16[160,128]{1,0:T(8,128)(2,1)S(1)}, bf16[160,128]{1,0:T(8,128)(2,1)}, u32[]{:S(2)}) copy-start(bf16[160,128]{1,0:T(8,128)(2,1)} %select_convert_fusion.3.hidden) | copy-start | bytes 122884
  383.3 9.6 %copy-start.2 = (f32[1024,640]{1,0:T(8,128)S(1)}, f32[1024,640]{1,0:T(8,128)}, u32[]{:S(2)}) copy-start(f32[1024,640]{1,0:T(8,128)} %get-tuple-element.164) | copy-start | bytes 7864324
  393.0 1.5 copy-start.7
  393.0 2.2 copy-start.8
  393.0 2.8 copy-start.6
  393.0 3.6 copy-start.5
  393.0 4.3 %copy-start.1 = (bf16[128,128]{1,0:T(8,128)(2,1)S(1)}, bf16[128,128]{1,0:T(8,128)(2,1)}, u32[]{:S(2)}) copy-start(bf16[128,128]{1,0:T(8,128)(2,1)} %param.27) | copy-start | bytes 98308
